TPU v7x, 512 devices: a whole 4x8x8 slice. The times are simulated.
512 devices in a mesh: pb: 16 (over y, core), ha: 32 (over z, x).
Axes of the slice: x: 4, y: 8, z: 8, core: 2. Of those that a mesh axis runs over, the one named last changes fastest.
Arguments:
- query_embed: bfloat16 [16384, 128], P(('pb', 'ha')), may hold values from -6 to 6
- host_embed: bfloat16 [65536, 128], P(('pb', 'ha')), may hold values from -6 to 6
- query_degree: int32 [16384], P(('pb', 'ha')), may hold values from 8 to 128
- host_degree: int32 [65536], P(('pb', 'ha')), may hold values from 8 to 128
- tile_rows: int32 [8192], P(('pb', 'ha')), may hold values from 0 to 127, as said below
- tile_cols: int32 [8192], P(('pb', 'ha')), may hold values from 0 to 511, as said below
- tile_counts: int32 [8192, 128, 128], P(('pb', 'ha')), may hold values from 0 to 3, as said below
- keep_mask: int32 [2, 8192], P(None, ('pb', 'ha')), may hold values 0 or 1
- live_tiles: int32 [512], P(('pb', 'ha')), may hold values from 4 to 16, as said below
Outputs:
- query_out: bfloat16 [2, 16384, 128], P(None, ('pb', 'ha'))
- host_out: bfloat16 [2, 65536, 128], P(None, ('pb', 'ha'))
Inputs may be any that keep to these rules, and one draw needn't show every extreme that they name: `tile_rows`: slot s of group d = s // 16 names a query block in [p * 8, (p + 1) * 8) with p = d // 32, for live and stale slots alike. `tile_cols`: slot s of group d = s // 16 names a host block c with c % 32 == d % 32, for live and stale slots alike. `tile_counts`: stale slots (at or past their group's live count) hold arbitrary counts. `live_tiles`: in every draw some slot group has all 16 slots live.
All inputs are finite; a program needn't handle non-finite values. No bound on the sum of `keep_mask` on one device may be relied on, other than what follows from the above.
Results may differ from a plain program's by a relative error of at most 0.02.
Values may be sent and summed in bfloat16 or wider, within the bound.
No kernel may reach another device: no remote copies, remote signals or barrier semaphores. Data moves between devices by JAX's collectives and lax.ppermute only.
A program may use at most 64 MiB of HBM per device.

v0:
```python
import jax
import jax.numpy as jnp
from jax import lax
from jax.sharding import PartitionSpec as P

DIM = 128
BLOCK = 128
LAYERS = 2


def tile_terms(weights, block_row, block_col, query_blocks, host_blocks):
    host_rows = jnp.take(host_blocks, block_col, axis=1)
    query_rows = jnp.take(query_blocks, block_row, axis=1)
    query_prod = jnp.einsum(
        "vtqh,vthw->vtqw", weights, host_rows, preferred_element_type=jnp.float32
    )
    host_prod = jnp.einsum(
        "vtqh,vtqw->vthw", weights, query_rows, preferred_element_type=jnp.float32
    )
    query_part = jnp.zeros(query_blocks.shape, jnp.float32).at[:, block_row].add(query_prod)
    host_part = jnp.zeros(host_blocks.shape, jnp.float32).at[:, block_col].add(host_prod)
    return (query_part, host_part)


def propagate_terms(weights, block_row, block_col, query_slab, host_group):
    query_blocks = query_slab.reshape(2, -1, BLOCK, DIM)
    host_blocks = host_group.reshape(2, -1, BLOCK, DIM)
    query_part, host_part = tile_terms(weights, block_row, block_col, query_blocks, host_blocks)
    return (query_part.reshape(2, -1, DIM), host_part.reshape(2, -1, DIM))


def collect(scale_query, scale_host, query_now, host_now):
    sent_query = (scale_query * query_now.astype(jnp.float32)).astype(jnp.bfloat16)
    sent_host = (scale_host * host_now.astype(jnp.float32)).astype(jnp.bfloat16)
    query_slab = lax.all_gather(sent_query, "ha", axis=1, tiled=True)
    host_group = lax.all_gather(sent_host, "pb", axis=1, tiled=True)
    return (query_slab, host_group)


def regroup(scale_query, scale_host, query_part, host_part):
    query_summed = lax.psum_scatter(
        query_part.astype(jnp.bfloat16), "ha", scatter_dimension=1, tiled=True
    ).astype(jnp.float32)
    host_summed = lax.psum_scatter(
        host_part.astype(jnp.bfloat16), "pb", scatter_dimension=1, tiled=True
    ).astype(jnp.float32)
    query_next = (scale_query * query_summed).astype(jnp.bfloat16)
    host_next = (scale_host * host_summed).astype(jnp.bfloat16)
    return (query_next, host_next)


def per_device(
    query_embed,
    host_embed,
    query_degree,
    host_degree,
    tile_rows,
    tile_cols,
    tile_counts,
    keep_mask,
    live_tiles,
):
    query_local = query_embed.shape[0]
    slab_blocks = lax.axis_size("ha") * query_local // BLOCK
    block_row = tile_rows - lax.axis_index("pb") * slab_blocks
    block_col = tile_cols // lax.axis_size("ha")
    live_count = live_tiles[0]
    slot_live = (jnp.arange(tile_rows.shape[0], dtype=jnp.int32) < live_count).astype(jnp.int32)
    weights = (tile_counts[None] * (keep_mask * slot_live[None])[:, :, None, None]).astype(
        jnp.bfloat16
    )
    scale_query = lax.rsqrt(query_degree.astype(jnp.float32))[:, None]
    scale_host = lax.rsqrt(host_degree.astype(jnp.float32))[:, None]
    query_now = jnp.stack([query_embed, query_embed])
    host_now = jnp.stack([host_embed, host_embed])
    query_total = query_now.astype(jnp.float32)
    host_total = host_now.astype(jnp.float32)
    for layer_index in range(LAYERS):
        query_slab, host_group = collect(scale_query, scale_host, query_now, host_now)
        query_part, host_part = propagate_terms(
            weights, block_row, block_col, query_slab, host_group
        )
        query_now, host_now = regroup(scale_query, scale_host, query_part, host_part)
        query_total = query_total + query_now.astype(jnp.float32)
        host_total = host_total + host_now.astype(jnp.float32)
    query_out = (query_total / (LAYERS + 1)).astype(jnp.bfloat16)
    host_out = (host_total / (LAYERS + 1)).astype(jnp.bfloat16)
    return (query_out, host_out)


def solution(mesh):
    in_specs = (
        P(("pb", "ha"), None),
        P(("pb", "ha"), None),
        P(("pb", "ha")),
        P(("pb", "ha")),
        P(("pb", "ha")),
        P(("pb", "ha")),
        P(("pb", "ha"), None, None),
        P(None, ("pb", "ha")),
        P(("pb", "ha")),
    )
    out_specs = (P(None, ("pb", "ha"), None), P(None, ("pb", "ha"), None))
    return jax.shard_map(
        per_device, mesh=mesh, in_specs=in_specs, out_specs=out_specs, check_vma=False
    )
```

profile of v0, /device:TPU:1, one launch (start us, length us, event | category | flops | bytes accessed | tf_op | source)
XLA Modules:
  0.0 782.3 jit_solution(1865639933149619962)
XLA Ops:
  7.9 1.6 fusion.20
  9.5 1.6 copy.14
  11.9 45.7 %all-gather.3.cloned.1.call-done = bf16[2,2048,128]{2,1,0:T(8,128)(2,1)} async-done(((bf16[2,128,128]{2,1,0:T(8,128)(2,1)}), bf16[2,2048,128]{2,1,0:T(8,128)(2,1)}) %all-gather.3.cloned.1.call-update) | async-done | bytes 1048592 | tf_op jit(solution)/shard_map/all_gather | solution.py:36
  57.5 2.0 gather_fusion
  59.5 0.8 fusion.4
  60.3 1.5 copy.17
  61.9 3.6 scatter_fusion
  65.5 0.9 convert_element_type.111
  66.5 213.0 %reduce-scatter.5.cloned.1.call-done = bf16[2,32,128]{2,1,0:T(8,128)(2,1)} async-done(((bf16[2,1024,128]{2,1,0:T(8,128)(2,1)}), bf16[2,32,128]{2,1,0:T(8,128)(2,1)}) %reduce-scatter.5.cloned.1.call-update) | async-done | bytes 16400 | tf_op jit(solution)/shard_map/reduce_scatter | solution.py:41
  279.5 0.8 fusion.29
  280.3 35.6 %all_gather.13 = bf16[2,1024,128]{2,1,0:T(8,128)(2,1)S(1)} all-gather(bf16[2,32,128]{2,1,0:T(8,128)(2,1)S(1)} %get-tuple-element.13), channel_id=1, replica_groups=mesh['pb'=16,'ha'=32] {'ha'}, dimensions={1}, use_global_device_ids=true | all-gather | bytes 540672 | tf_op jit(solution)/shard_map/all_gather | solution.py:35
  315.9 36.0 %all_gather.15 = bf16[2,1024,128]{2,1,0:T(8,128)(2,1)S(1)} all-gather(bf16[2,32,128]{2,1,0:T(8,128)(2,1)S(1)} %get-tuple-element.12), channel_id=1, replica_groups=mesh['pb'=16,'ha'=32] {'ha'}, dimensions={1}, use_global_device_ids=true | all-gather | bytes 540672 | tf_op jit(solution)/shard_map/all_gather | solution.py:35
  351.9 0.7 gather_fusion.1
  352.7 1.7 gather_fusion.3
  354.4 2.5 select_bitcast_fusion
  357.3 1.5 copy.19
  359.1 3.7 scatter_fusion.1
  362.7 1.2 convert_element_type.117
  364.0 1.7 fusion.7
  365.7 1.5 copy.24
  367.4 3.7 scatter_fusion.3
  371.1 1.1 convert_element_type.130
  372.3 76.5 %reduce-scatter.7.cloned.1.call-done = bf16[2,128,128]{2,1,0:T(8,128)(2,1)} async-done(((bf16[2,2048,128]{2,1,0:T(8,128)(2,1)}), bf16[2,128,128]{2,1,0:T(8,128)(2,1)}) %reduce-scatter.7.cloned.1.call-update) | async-done | bytes 65552 | tf_op jit(solution)/shard_map/reduce_scatter | solution.py:44
  448.8 61.5 %reduce-scatter.11.cloned.1.call-done = bf16[2,128,128]{2,1,0:T(8,128)(2,1)} async-done(((bf16[2,2048,128]{2,1,0:T(8,128)(2,1)}), bf16[2,128,128]{2,1,0:T(8,128)(2,1)}) %reduce-scatter.11.cloned.1.call-update) | async-done | bytes 65552 | tf_op jit(solution)/shard_map/reduce_scatter | solution.py:44
  510.2 1.6 fusion.24
  512.1 42.6 %all-gather.5.cloned.1.call-done = bf16[2,2048,128]{2,1,0:T(8,128)(2,1)} async-done(((bf16[2,128,128]{2,1,0:T(8,128)(2,1)}), bf16[2,2048,128]{2,1,0:T(8,128)(2,1)}) %all-gather.5.cloned.1.call-update) | async-done | bytes 1048592 | tf_op jit(solution)/shard_map/all_gather | solution.py:36
  554.7 2.0 gather_fusion.2
  556.7 0.8 fusion.6
  557.7 2.3 scatter_fusion.2
  560.0 0.9 convert_element_type.123
  560.9 213.1 %reduce-scatter.9.cloned.1.call-done = bf16[2,32,128]{2,1,0:T(8,128)(2,1)} async-done(((bf16[2,1024,128]{2,1,0:T(8,128)(2,1)}), bf16[2,32,128]{2,1,0:T(8,128)(2,1)}) %reduce-scatter.9.cloned.1.call-update) | async-done | bytes 16400 | tf_op jit(solution)/shard_map/reduce_scatter | solution.py:41
  774.0 1.4 fusion.28
  (40 shorter events, 2.6 us)
Async XLA Ops:
  7.2 4.6 copy-start.5
  7.2 4.6 copy-start.4
  7.2 4.7 copy-start.3
  7.2 50.3 %all-gather.3.cloned.1.call-start = ((), (), s32[]{:S(2)}) async-start(), calls=%async_computation.4 | async-start | bytes 1114112 | tf_op jit(solution)/shard_map/all_gather | solution.py:36
  9.5 270.1 %reduce-scatter.5.cloned.1.call-start = ((), (), s32[]{:S(2)}) async-start(), calls=%async_computation.5 | async-start | bytes 540672 | tf_op jit(solution)/shard_map/reduce_scatter | solution.py:41
  65.5 1.0 copy-start.6
  65.5 214.0 %copy-start.2 = (bf16[32,128]{1,0:T(8,128)(2,1)S(1)}, bf16[32,128]{1,0:T(8,128)(2,1)}, u32[]{:S(2)}) copy-start(bf16[32,128]{1,0:T(8,128)(2,1)} %param.13) | copy-start | bytes 24580
  66.4 382.4 %reduce-scatter.7.cloned.1.call-start = ((), (), s32[]{:S(2)}) async-start(), calls=%async_computation.6 | async-start | bytes 1114112 | tf_op jit(solution)/shard_map/reduce_scatter | solution.py:44
  363.9 146.3 %reduce-scatter.11.cloned.1.call-start = ((), (), s32[]{:S(2)}) async-start(), calls=%async_computation.9 | async-start | bytes 1114112 | tf_op jit(solution)/shard_map/reduce_scatter | solution.py:44
  371.1 139.1 %copy-start = (bf16[128,128]{1,0:T(8,128)(2,1)S(1)}, bf16[128,128]{1,0:T(8,128)(2,1)}, u32[]{:S(2)}) copy-start(bf16[128,128]{1,0:T(8,128)(2,1)} %param.14) | copy-start | bytes 98308
  372.3 182.4 %all-gather.5.cloned.1.call-start = ((), (), s32[]{:S(2)}) async-start(), calls=%async_computation.7 | async-start | bytes 1114112 | tf_op jit(solution)/shard_map/all_gather | solution.py:36
  511.9 262.1 %reduce-scatter.9.cloned.1.call-start = ((), (), s32[]{:S(2)}) async-start(), calls=%async_computation.8 | async-start | bytes 540672 | tf_op jit(solution)/shard_map/reduce_scatter | solution.py:41
  560.0 214.0 %copy-start.1 = (bf16[2,32,128]{2,1,0:T(8,128)(2,1)S(1)}, bf16[2,32,128]{2,1,0:T(8,128)(2,1)}, u32[]{:S(2)}) copy-start(bf16[2,32,128]{2,1,0:T(8,128)(2,1)} %reduce-scatter.5.cloned.1.call-done) | copy-start | bytes 49156
Sparse Core Ops, SparseCore 0:
  10.7 46.7 all-gather.2
  66.5 212.9 reduce-scatter.4
  364.1 84.6 reduce-scatter.6
  451.4 58.7 reduce-scatter.10
  512.4 42.1 all-gather.4
  561.1 212.9 reduce-scatter.8
where the time goes:
time: 787 us; the launch traced here: 782 us
  waiting for transfers between devices  652 us (83%)
  blocking collectives  71.6 us (9%)
  other arithmetic  25.9 us (3%)
  between operations  15 us (2%)
  local copies, waits for them, and re-layouts  13.2 us (2%)
    reduce_scatter x2, waiting for transfers between devices, regroup(): lax.psum_scatter(query_part.astype(jnp.bfloat16), 'ha', scatter_dimension...  426 us
    reduce_scatter x2, waiting for transfers between devices, regroup(): lax.psum_scatter(host_part.astype(jnp.bfloat16), 'pb', scatter_dimension=...  138 us
    all_gather x2, waiting for transfers between devices, collect(): host_group = lax.all_gather(sent_host, 'pb', axis=1, tiled=True)  88.2 us
    all_gather x2, blocking collectives, collect(): query_slab = lax.all_gather(sent_query, 'ha', axis=1, tiled=True)  71.6 us
  transfers between devices with their start and end apart: 6, of which 6 were waited for; matrix products, arithmetic and copies ran while one was open for 1% of the time, Pallas kernels for 0%

commit v1 on v0

v1 whole, which is shorter than its diff:
```python
import functools

import jax
import jax.numpy as jnp
from jax import lax
from jax.experimental import pallas as pl
from jax.experimental.pallas import tpu as pltpu
from jax.sharding import PartitionSpec as P

DIM = 128
BLOCK = 128
CAP = 16
LAYERS = 2
BOTH = 2 * DIM

SMEM = pl.BlockSpec(memory_space=pltpu.SMEM)
VMEM = pl.BlockSpec(memory_space=pltpu.VMEM)


def add_views(acc_ref, slot, keep_ref, s, prod):
    first = prod[:, :DIM]
    second = prod[:, -DIM:]
    acc_ref[slot, :, :DIM] += keep_ref[0, s] * first
    acc_ref[slot, :, DIM:] += keep_ref[1, s] * second


def host_kernel(
    rows_ref, slots_ref, keep_ref, w_ref, q_ref, own_ref, send_ref, acc_ref
):
    acc_ref[...] = jnp.zeros_like(acc_ref)
    for s in range(CAP):
        at = pl.multiple_of(rows_ref[s] * BLOCK, BLOCK)
        prod = lax.dot_general(
            w_ref[s],
            q_ref[pl.ds(at, BLOCK), :],
            (((0,), (0,)), ((), ())),
            preferred_element_type=jnp.float32,
        )
        add_views(acc_ref, slots_ref[s], keep_ref, s, prod)
    half = acc_ref.shape[0] // 2
    own_ref[...] = acc_ref[:half]
    send_ref[...] = acc_ref[half:].astype(jnp.bfloat16)


def pick(pieces, slot, width):
    size = pieces[0].shape[0] // BLOCK
    at = pl.multiple_of((slot % size) * BLOCK, BLOCK)
    block = pieces[0][pl.ds(at, BLOCK), :width]
    if len(pieces) == 2:
        block = jnp.where(slot < size, block, pieces[1][pl.ds(at, BLOCK), :width])
    return block


def query_kernel(
    rows_ref, cols_ref, keep_ref, w_ref, *refs, width
):
    *pieces, part_ref, acc_ref = refs
    acc_ref[...] = jnp.zeros_like(acc_ref)
    for s in range(CAP):
        host = pick(pieces, cols_ref[s], width)
        prod = jnp.dot(w_ref[s], host, preferred_element_type=jnp.float32)
        add_views(acc_ref, rows_ref[s], keep_ref, s, prod)
    part_ref[...] = acc_ref[...].astype(jnp.bfloat16)


def cost(width):
    return pl.CostEstimate(
        flops=2 * CAP * BLOCK * BLOCK * width, bytes_accessed=3 * 2**20, transcendentals=0
    )


def host_sums(rows, slots, keep, weights, slab, blocks):
    half = blocks // 2
    return pl.pallas_call(
        host_kernel,
        out_shape=(
            jax.ShapeDtypeStruct((half, BLOCK, BOTH), jnp.float32),
            jax.ShapeDtypeStruct((half, BLOCK, BOTH), jnp.bfloat16),
        ),
        in_specs=[SMEM, SMEM, SMEM, VMEM, VMEM],
        out_specs=(VMEM, VMEM),
        scratch_shapes=[pltpu.VMEM((blocks, BLOCK, BOTH), jnp.float32)],
        cost_estimate=cost(slab.shape[1]),
        compiler_params=pltpu.CompilerParams(vmem_limit_bytes=24 * 2**20),
        name="host_sums",
    )(rows, slots, keep, weights, slab)


def query_sums(rows, cols, keep, weights, pieces, blocks, width):
    return pl.pallas_call(
        functools.partial(query_kernel, width=width),
        out_shape=jax.ShapeDtypeStruct((blocks, BLOCK, BOTH), jnp.bfloat16),
        in_specs=[SMEM, SMEM, SMEM] + [VMEM] * (1 + len(pieces)),
        out_specs=VMEM,
        scratch_shapes=[pltpu.VMEM((blocks, BLOCK, BOTH), jnp.float32)],
        cost_estimate=cost(width),
        compiler_params=pltpu.CompilerParams(vmem_limit_bytes=24 * 2**20),
        name="query_sums",
    )(rows, cols, keep, weights, *pieces)


def exchange(blocks, axis, groups=None):
    return lax.all_to_all(blocks, axis, 0, 0, axis_index_groups=groups, tiled=True)


def spread(local, axis):
    size = lax.axis_size(axis)
    copies = jnp.broadcast_to(local[None], (size,) + local.shape)
    return exchange(copies, axis).reshape(size * local.shape[0], local.shape[1])


def split_views(both):
    return jnp.stack([both[:, :DIM], both[:, DIM:]])


def per_device(
    query_embed,
    host_embed,
    query_degree,
    host_degree,
    tile_rows,
    tile_cols,
    tile_counts,
    keep_mask,
    live_tiles,
):
    n_pb, n_ha = lax.axis_size("pb"), lax.axis_size("ha")
    query_local = query_embed.shape[0]
    slab_blocks = n_ha * query_local // BLOCK
    chips = n_pb // 2
    core = lax.axis_index("pb") % 2
    same_core = [[2 * y + c for y in range(chips)] for c in range(2)]
    other_core = [(i, i ^ 1) for i in range(n_pb)]

    rows = tile_rows % slab_blocks
    cols = tile_cols // n_ha
    slots = ((cols % 2) ^ core) * chips + cols // 2
    live = jnp.arange(CAP, dtype=jnp.int32) < live_tiles[0]
    keep = (keep_mask * live[None]).astype(jnp.float32)
    weights = tile_counts.astype(jnp.bfloat16)
    scale_query = lax.rsqrt(query_degree.astype(jnp.float32))[:, None]
    scale_host = lax.rsqrt(host_degree.astype(jnp.float32))[:, None]

    def sent(scale, now):
        return (scale * now.astype(jnp.float32)).astype(jnp.bfloat16)

    def reduce_query(part):
        pieces = exchange(part.reshape(n_ha, query_local, BOTH), "ha")
        return sent(scale_query, jnp.sum(pieces.astype(jnp.float32), axis=0))

    def pair_host(own, send):
        other = lax.ppermute(send, "pb", other_core)
        return (own + other.astype(jnp.float32)).astype(jnp.bfloat16)

    def reduce_host(pair):
        pieces = exchange(pair, "pb", same_core)
        return sent(scale_host, jnp.sum(pieces.astype(jnp.float32), axis=0))

    def gather_host(local):
        copies = jnp.broadcast_to(local[None], (chips,) + local.shape)
        mine = exchange(copies, "pb", same_core).reshape(chips * BLOCK, local.shape[1])
        return mine, lax.ppermute(mine, "pb", other_core)

    slab = spread(sent(scale_query, query_embed), "ha")
    pieces = gather_host(sent(scale_host, host_embed))
    own, send = host_sums(rows, slots, keep, weights, slab, n_pb)
    pair = pair_host(own, send)
    host_1 = reduce_host(pair)
    sent_host = sent(scale_host, host_1)
    part = query_sums(rows, slots, keep, weights, pieces, slab_blocks, DIM)
    query_1 = reduce_query(part)

    pieces = gather_host(sent_host)
    slab = spread(sent(scale_query, query_1), "ha")
    own, send = host_sums(rows, slots, keep, weights, slab, n_pb)
    pair = pair_host(own, send)
    host_2 = reduce_host(pair)
    part = query_sums(rows, slots, keep, weights, pieces, slab_blocks, BOTH)
    query_2 = reduce_query(part)

    def mean(embed, one, two):
        zero = embed.astype(jnp.float32)[None]
        total = zero + split_views(one).astype(jnp.float32) + split_views(two).astype(jnp.float32)
        return (total / (LAYERS + 1)).astype(jnp.bfloat16)

    return (mean(query_embed, query_1, query_2), mean(host_embed, host_1, host_2))


def solution(mesh):
    in_specs = (
        P(("pb", "ha"), None),
        P(("pb", "ha"), None),
        P(("pb", "ha")),
        P(("pb", "ha")),
        P(("pb", "ha")),
        P(("pb", "ha")),
        P(("pb", "ha"), None, None),
        P(None, ("pb", "ha")),
        P(("pb", "ha")),
    )
    out_specs = (P(None, ("pb", "ha"), None), P(None, ("pb", "ha"), None))
    return jax.shard_map(
        per_device, mesh=mesh, in_specs=in_specs, out_specs=out_specs, check_vma=False
    )
```

time: 787 us -> 186 us (0.24)
  waiting for transfers between devices: 652 us -> 77.4 us
  starting transfers between devices: 0.43 us -> 74.9 us
  blocking collectives: 71.6 us -> 14.7 us
  other arithmetic: 25.9 us -> 6.69 us
  between operations: 15 us -> 1.55 us
  local copies, waits for them, and re-layouts: 13.2 us -> 3.04 us
    reduce_scatter x4 -> x0, waiting for transfers between devices: 564 us -> none  [the longest x2 426 us: regroup(): lax.psum_scatter(query_part.astype(jnp.bfloat16), 'ha', scatter_dimension...]
    all_gather x2 -> x0, waiting for transfers between devices: 88.2 us -> none  [collect(): host_group = lax.all_gather(sent_host, 'pb', axis=1, tiled=True)]
    all_to_all x0 -> x7, waiting for transfers between devices: none -> 72.8 us  [exchange(): lax.all_to_all(blocks, axis, 0, 0, axis_index_groups=groups, tiled=True)]
    all_gather x2 -> x0, blocking collectives: 71.6 us -> none  [collect(): query_slab = lax.all_gather(sent_query, 'ha', axis=1, tiled=True)]
    all_to_all x0 -> x7, starting transfers between devices: none -> 49.9 us  [exchange(): lax.all_to_all(blocks, axis, 0, 0, axis_index_groups=groups, tiled=True)]
    ppermute x0 -> x4, starting transfers between devices: none -> 25 us  [the longest x2 14.8 us: gather_host(): return (mine, lax.ppermute(mine, 'pb', other_core))]
    all_to_all x0 -> x1, blocking collectives: none -> 14.7 us  [exchange(): lax.all_to_all(blocks, axis, 0, 0, axis_index_groups=groups, tiled=True)]
    scatter-add x4 -> x0, other arithmetic: 13.2 us -> none  [the longest x2 7.32 us: tile_terms(): jnp.zeros(host_blocks.shape, jnp.float32).at[:, block_col].add(host_prod)]
  transfers between devices with their start and end apart: 6 -> 11, of which waited for: 6 -> 10; matrix products, arithmetic and copies ran while one was open for 1% -> 2% of each run, Pallas kernels for 0% -> 1%
where the time goes in v1:
time: 186 us; the launch traced here: 184 us
  waiting for transfers between devices  77.4 us (42%)
  starting transfers between devices  74.9 us (40%)
  blocking collectives  14.7 us (8%)
  other arithmetic  6.69 us (4%)
  Pallas kernels  6.17 us (3%)
  local copies, waits for them, and re-layouts  3.04 us (2%)
    all_to_all x7, waiting for transfers between devices, exchange(): lax.all_to_all(blocks, axis, 0, 0, axis_index_groups=groups, tiled=True)  72.8 us
    all_to_all x7, starting transfers between devices, exchange(): lax.all_to_all(blocks, axis, 0, 0, axis_index_groups=groups, tiled=True)  49.9 us
    ppermute x2, starting transfers between devices, gather_host(): return (mine, lax.ppermute(mine, 'pb', other_core))  14.8 us
    all_to_all x1, blocking collectives, exchange(): lax.all_to_all(blocks, axis, 0, 0, axis_index_groups=groups, tiled=True)  14.7 us
    ppermute x2, starting transfers between devices, pair_host(): other = lax.ppermute(send, 'pb', other_core)  10.2 us
    pallas_call x2, Pallas kernels, query_sums(): pl.pallas_call(functools.partial(query_kernel, width=width), out_shape=ja...  3.77 us
  transfers between devices with their start and end apart: 11, of which 10 were waited for; matrix products, arithmetic and copies ran while one was open for 2% of the time, Pallas kernels for 1%

profile of v1, /device:TPU:1, one launch (start us, length us, event | category | flops | bytes accessed | tf_op | source)
XLA Modules:
  0.0 184.5 jit_solution(10009464058864844655)
XLA Ops:
  1.3 0.8 multiply_convert_fusion.4
  2.1 0.7 broadcast_in_dim.8
  2.9 7.7 %all-to-all-start = ((bf16[8,128,128]{2,1,0:T(8,128)(2,1)}), bf16[8,128,128]{2,1,0:T(8,128)(2,1)S(1)}, u32[]{:S(2)}, u32[]{:S(2)}) async-start(bf16[8,128,128]{2,1,0:T(8,128)(2,1)} %broadcast_in_dim.8), calls=%async_computation | async-start | bytes 524288 | tf_op jit(solution)/shard_map/all_to_all | solution.py:103
  11.9 8.1 %all-to-all-done = bf16[8,128,128]{2,1,0:T(8,128)(2,1)S(1)} async-done(((bf16[8,128,128]{2,1,0:T(8,128)(2,1)}), bf16[8,128,128]{2,1,0:T(8,128)(2,1)S(1)}, u32[]{:S(2)}, u32[]{:S(2)}) %all-to-all-start) | async-done | bytes 262176 | tf_op jit(solution)/shard_map/all_to_all | solution.py:103
  19.9 5.5 %collective-permute-start = (bf16[1024,128]{1,0:T(8,128)(2,1)S(1)}, bf16[1024,128]{1,0:T(8,128)(2,1)S(1)}, u32[]{:S(2)}, u32[]{:S(2)}) collective-permute-start(bf16[1024,128]{1,0:T(8,128)(2,1)S(1)} %bitcast.28), channel_id=1, source_target_pairs={{0,32},{32,0},{64,96},{96,64},{128,160},{160,128},{192,224},{224,1... | collective-permute-start | bytes 786440 | tf_op jit(solution)/shard_map/ppermute | solution.py:162
  25.5 1.3 convert_element_type.128.w_ref
  26.9 1.9 %query_sums.2 = bf16[8,128,256]{2,1,0:T(8,128)(2,1)} custom-call(s32[16]{0:T(128)S(1)} %get-tuple-element.23.rows_ref, s32[16]{0:T(128)S(1)} %get-tuple-element.24.cols_ref.slots_ref, f32[2,16]{1,0:T(2,128)S(1)} %multiply_convert_fusion.10.keep_ref, bf16[16,128,128]{2,1,0:T(8,128)(2,1)S(1)} %convert_element_type.128.w_ref, bf16[1024,128]{1,0:T(8,128)(2,1)S(1)} %bitcast.29, ...), custom_call_target="tpu_custom_call" | custom-call | flops 67108864 | bytes 3145728 | tf_op jit(solution)/shard_map/query_sums/pallas_call | solution.py:90
  28.7 12.8 %all-to-all-start.1 = ((bf16[32,32,256]{2,1,0:T(8,128)(2,1)}), bf16[32,32,256]{2,1,0:T(8,128)(2,1)S(1)}, u32[]{:S(2)}, u32[]{:S(2)}) async-start(bf16[32,32,256]{2,1,0:T(8,128)(2,1)} %bitcast.2), calls=%async_computation.1 | async-start | bytes 1048576 | tf_op jit(solution)/shard_map/all_to_all | solution.py:103
  41.7 16.7 %all-to-all-done.1 = bf16[32,32,256]{2,1,0:T(8,128)(2,1)S(1)} async-done(((bf16[32,32,256]{2,1,0:T(8,128)(2,1)}), bf16[32,32,256]{2,1,0:T(8,128)(2,1)S(1)}, u32[]{:S(2)}, u32[]{:S(2)}) %all-to-all-start.1) | async-done | bytes 524320 | tf_op jit(solution)/shard_map/all_to_all | solution.py:103
  59.1 5.0 %all-to-all-start.2 = ((bf16[32,32,128]{2,1,0:T(8,128)(2,1)}), bf16[32,32,128]{2,1,0:T(8,128)(2,1)S(1)}, u32[]{:S(2)}, u32[]{:S(2)}) async-start(bf16[32,32,128]{2,1,0:T(8,128)(2,1)} %broadcast_in_dim.9), calls=%async_computation.2 | async-start | bytes 524288 | tf_op jit(solution)/shard_map/all_to_all | solution.py:103
  64.2 10.3 %all-to-all-done.2 = bf16[32,32,128]{2,1,0:T(8,128)(2,1)S(1)} async-done(((bf16[32,32,128]{2,1,0:T(8,128)(2,1)}), bf16[32,32,128]{2,1,0:T(8,128)(2,1)S(1)}, u32[]{:S(2)}, u32[]{:S(2)}) %all-to-all-start.2) | async-done | bytes 262176 | tf_op jit(solution)/shard_map/all_to_all | solution.py:103
  74.5 0.8 broadcast_in_dim.11
  75.3 5.2 %all-to-all-start.6 = ((bf16[32,32,256]{2,1,0:T(8,128)(2,1)}), bf16[32,32,256]{2,1,0:T(8,128)(2,1)S(1)}, u32[]{:S(2)}, u32[]{:S(2)}) async-start(bf16[32,32,256]{2,1,0:T(8,128)(2,1)} %broadcast_in_dim.11), calls=%async_computation.6 | async-start | bytes 1048576 | tf_op jit(solution)/shard_map/all_to_all | solution.py:103
  80.6 1.2 host_sums.2
  81.8 4.1 %collective-permute-start.1 = (bf16[8,128,256]{2,1,0:T(8,128)(2,1)S(1)}, bf16[8,128,256]{2,1,0:T(8,128)(2,1)S(1)}, u32[]{:S(2)}, u32[]{:S(2)}) collective-permute-start(bf16[8,128,256]{2,1,0:T(8,128)(2,1)S(1)} %get-tuple-element.7), channel_id=1, source_target_pairs={{0,32},{32,0},{64,96},{96,64},{128,160},{160,128},{192,224},{224,1... | collective-permute-start | bytes 1572872 | tf_op jit(solution)/shard_map/ppermute | solution.py:152
  85.9 1.5 collective-permute-done.1
  87.4 1.0 add_convert_fusion.1
  88.3 6.9 %all-to-all-done.6 = bf16[32,32,256]{2,1,0:T(8,128)(2,1)S(1)} async-done(((bf16[32,32,256]{2,1,0:T(8,128)(2,1)}), bf16[32,32,256]{2,1,0:T(8,128)(2,1)S(1)}, u32[]{:S(2)}, u32[]{:S(2)}) %all-to-all-start.6) | async-done | bytes 524320 | tf_op jit(solution)/shard_map/all_to_all | solution.py:103
  95.2 3.5 %all-to-all-start.3 = ((bf16[8,128,256]{2,1,0:T(8,128)(2,1)}), bf16[8,128,256]{2,1,0:T(8,128)(2,1)S(1)}, u32[]{:S(2)}, u32[]{:S(2)}) async-start(bf16[8,128,256]{2,1,0:T(8,128)(2,1)} %add_convert_fusion.1), calls=%async_computation.3 | async-start | bytes 1048576 | tf_op jit(solution)/shard_map/all_to_all | solution.py:103
  98.7 1.2 host_sums.3
  100.0 6.1 %collective-permute-start.3 = (bf16[8,128,256]{2,1,0:T(8,128)(2,1)S(1)}, bf16[8,128,256]{2,1,0:T(8,128)(2,1)S(1)}, u32[]{:S(2)}, u32[]{:S(2)}) collective-permute-start(bf16[8,128,256]{2,1,0:T(8,128)(2,1)S(1)} %get-tuple-element.9), channel_id=1, source_target_pairs={{0,32},{32,0},{64,96},{96,64},{128,160},{160,128},{192,224},{224,1... | collective-permute-start | bytes 1572872 | tf_op jit(solution)/shard_map/ppermute | solution.py:152
  106.0 1.5 collective-permute-done.3
  107.5 0.9 add_convert_fusion
  108.5 3.1 %all-to-all-done.3 = bf16[8,128,256]{2,1,0:T(8,128)(2,1)S(1)} async-done(((bf16[8,128,256]{2,1,0:T(8,128)(2,1)}), bf16[8,128,256]{2,1,0:T(8,128)(2,1)S(1)}, u32[]{:S(2)}, u32[]{:S(2)}) %all-to-all-start.3) | async-done | bytes 524320 | tf_op jit(solution)/shard_map/all_to_all | solution.py:103
  111.6 3.7 %all-to-all-start.7 = ((bf16[8,128,256]{2,1,0:T(8,128)(2,1)}), bf16[8,128,256]{2,1,0:T(8,128)(2,1)S(1)}, u32[]{:S(2)}, u32[]{:S(2)}) async-start(bf16[8,128,256]{2,1,0:T(8,128)(2,1)} %add_convert_fusion), calls=%async_computation.7 | async-start | bytes 1048576 | tf_op jit(solution)/shard_map/all_to_all | solution.py:103
  115.4 12.0 %all-to-all-done.7 = bf16[8,128,256]{2,1,0:T(8,128)(2,1)S(1)} async-done(((bf16[8,128,256]{2,1,0:T(8,128)(2,1)}), bf16[8,128,256]{2,1,0:T(8,128)(2,1)S(1)}, u32[]{:S(2)}, u32[]{:S(2)}) %all-to-all-start.7) | async-done | bytes 524320 | tf_op jit(solution)/shard_map/all_to_all | solution.py:103
  127.7 14.7 %all_to_all.40 = bf16[8,128,256]{2,1,0:T(8,128)(2,1)S(1)} all-to-all(bf16[8,128,256]{2,1,0:T(8,128)(2,1)S(1)} %broadcast_in_dim.10), channel_id=1, replica_groups={{0,64,128,192,256,320,384,448},{32,96,160,224,288,352,416,480},{1,65,12..., dimensions={0} | all-to-all | bytes 1048576 | tf_op jit(solution)/shard_map/all_to_all | solution.py:103
  142.4 9.3 %collective-permute-start.2 = (bf16[1024,256]{1,0:T(8,128)(2,1)S(1)}, bf16[1024,256]{1,0:T(8,128)(2,1)S(1)}, u32[]{:S(2)}, u32[]{:S(2)}) collective-permute-start(bf16[1024,256]{1,0:T(8,128)(2,1)S(1)} %bitcast.24), channel_id=1, source_target_pairs={{0,32},{32,0},{64,96},{96,64},{128,160},{160,128},{192,224},{224,1... | collective-permute-start | bytes 1572872 | tf_op jit(solution)/shard_map/ppermute | solution.py:162
  151.7 1.5 collective-permute-done.2.refs_1_
  153.2 1.9 %query_sums.3 = bf16[8,128,256]{2,1,0:T(8,128)(2,1)} custom-call(s32[16]{0:T(128)S(1)} %get-tuple-element.23.rows_ref, s32[16]{0:T(128)S(1)} %get-tuple-element.24.cols_ref.slots_ref, f32[2,16]{1,0:T(2,128)S(1)} %multiply_convert_fusion.10.keep_ref, bf16[16,128,128]{2,1,0:T(8,128)(2,1)S(1)} %convert_element_type.128.w_ref, bf16[1024,256]{1,0:T(8,128)(2,1)S(1)} %bitcast.25, ...), custom_call_target="tpu_custom_call" | custom-call | flops 134217728 | bytes 3145728 | tf_op jit(solution)/shard_map/query_sums/pallas_call | solution.py:90
  155.1 12.0 %all-to-all-start.5 = ((bf16[32,32,256]{2,1,0:T(8,128)(2,1)}), bf16[32,32,256]{2,1,0:T(8,128)(2,1)S(1)}, u32[]{:S(2)}, u32[]{:S(2)}) async-start(bf16[32,32,256]{2,1,0:T(8,128)(2,1)} %bitcast.7), calls=%async_computation.5 | async-start | bytes 1048576 | tf_op jit(solution)/shard_map/all_to_all | solution.py:103
  167.8 15.8 %all-to-all-done.5 = bf16[32,32,256]{2,1,0:T(8,128)(2,1)S(1)} async-done(((bf16[32,32,256]{2,1,0:T(8,128)(2,1)}), bf16[32,32,256]{2,1,0:T(8,128)(2,1)S(1)}, u32[]{:S(2)}, u32[]{:S(2)}) %all-to-all-start.5) | async-done | bytes 524320 | tf_op jit(solution)/shard_map/all_to_all | solution.py:103
  (36 shorter events, 4.1 us)
Async XLA Ops:
  2.9 17.1 %all-to-all-start = ((bf16[8,128,128]{2,1,0:T(8,128)(2,1)}), bf16[8,128,128]{2,1,0:T(8,128)(2,1)S(1)}, u32[]{:S(2)}, u32[]{:S(2)}) async-start(bf16[8,128,128]{2,1,0:T(8,128)(2,1)} %broadcast_in_dim.8), calls=%async_computation | async-start | bytes 524288 | tf_op jit(solution)/shard_map/all_to_all | solution.py:103
  11.2 0.7 copy-start.3
  11.2 0.7 copy-start.4
  19.9 6.9 %collective-permute-start = (bf16[1024,128]{1,0:T(8,128)(2,1)S(1)}, bf16[1024,128]{1,0:T(8,128)(2,1)S(1)}, u32[]{:S(2)}, u32[]{:S(2)}) collective-permute-start(bf16[1024,128]{1,0:T(8,128)(2,1)S(1)} %bitcast.28), channel_id=1, source_target_pairs={{0,32},{32,0},{64,96},{96,64},{128,160},{160,128},{192,224},{224,1... | collective-permute-start | bytes 786440 | tf_op jit(solution)/shard_map/ppermute | solution.py:162
  25.5 1.4 copy-start.2
  28.7 12.8 %copy-start.5 = (s32[32]{0:T(128)S(1)}, s32[32]{0:T(128)}, u32[]{:S(2)}) copy-start(s32[32]{0:T(128)} %param.11) | copy-start | bytes 388
  28.7 12.9 %copy-start.1 = (bf16[32,128]{1,0:T(8,128)(2,1)S(1)}, bf16[32,128]{1,0:T(8,128)(2,1)}, u32[]{:S(2)}) copy-start(bf16[32,128]{1,0:T(8,128)(2,1)} %param.9) | copy-start | bytes 24580
  28.7 29.6 %all-to-all-start.1 = ((bf16[32,32,256]{2,1,0:T(8,128)(2,1)}), bf16[32,32,256]{2,1,0:T(8,128)(2,1)S(1)}, u32[]{:S(2)}, u32[]{:S(2)}) async-start(bf16[32,32,256]{2,1,0:T(8,128)(2,1)} %bitcast.2), calls=%async_computation.1 | async-start | bytes 1048576 | tf_op jit(solution)/shard_map/all_to_all | solution.py:103
  59.1 15.4 %all-to-all-start.2 = ((bf16[32,32,128]{2,1,0:T(8,128)(2,1)}), bf16[32,32,128]{2,1,0:T(8,128)(2,1)S(1)}, u32[]{:S(2)}, u32[]{:S(2)}) async-start(bf16[32,32,128]{2,1,0:T(8,128)(2,1)} %broadcast_in_dim.9), calls=%async_computation.2 | async-start | bytes 524288 | tf_op jit(solution)/shard_map/all_to_all | solution.py:103
  75.3 19.9 %all-to-all-start.6 = ((bf16[32,32,256]{2,1,0:T(8,128)(2,1)}), bf16[32,32,256]{2,1,0:T(8,128)(2,1)S(1)}, u32[]{:S(2)}, u32[]{:S(2)}) async-start(bf16[32,32,256]{2,1,0:T(8,128)(2,1)} %broadcast_in_dim.11), calls=%async_computation.6 | async-start | bytes 1048576 | tf_op jit(solution)/shard_map/all_to_all | solution.py:103
  81.8 5.6 %collective-permute-start.1 = (bf16[8,128,256]{2,1,0:T(8,128)(2,1)S(1)}, bf16[8,128,256]{2,1,0:T(8,128)(2,1)S(1)}, u32[]{:S(2)}, u32[]{:S(2)}) collective-permute-start(bf16[8,128,256]{2,1,0:T(8,128)(2,1)S(1)} %get-tuple-element.7), channel_id=1, source_target_pairs={{0,32},{32,0},{64,96},{96,64},{128,160},{160,128},{192,224},{224,1... | collective-permute-start | bytes 1572872 | tf_op jit(solution)/shard_map/ppermute | solution.py:152
  95.2 16.4 %all-to-all-start.3 = ((bf16[8,128,256]{2,1,0:T(8,128)(2,1)}), bf16[8,128,256]{2,1,0:T(8,128)(2,1)S(1)}, u32[]{:S(2)}, u32[]{:S(2)}) async-start(bf16[8,128,256]{2,1,0:T(8,128)(2,1)} %add_convert_fusion.1), calls=%async_computation.3 | async-start | bytes 1048576 | tf_op jit(solution)/shard_map/all_to_all | solution.py:103
  100.0 7.6 %collective-permute-start.3 = (bf16[8,128,256]{2,1,0:T(8,128)(2,1)S(1)}, bf16[8,128,256]{2,1,0:T(8,128)(2,1)S(1)}, u32[]{:S(2)}, u32[]{:S(2)}) collective-permute-start(bf16[8,128,256]{2,1,0:T(8,128)(2,1)S(1)} %get-tuple-element.9), channel_id=1, source_target_pairs={{0,32},{32,0},{64,96},{96,64},{128,160},{160,128},{192,224},{224,1... | collective-permute-start | bytes 1572872 | tf_op jit(solution)/shard_map/ppermute | solution.py:152
  111.6 15.8 %all-to-all-start.7 = ((bf16[8,128,256]{2,1,0:T(8,128)(2,1)}), bf16[8,128,256]{2,1,0:T(8,128)(2,1)S(1)}, u32[]{:S(2)}, u32[]{:S(2)}) async-start(bf16[8,128,256]{2,1,0:T(8,128)(2,1)} %add_convert_fusion), calls=%async_computation.7 | async-start | bytes 1048576 | tf_op jit(solution)/shard_map/all_to_all | solution.py:103
  142.4 10.8 %collective-permute-start.2 = (bf16[1024,256]{1,0:T(8,128)(2,1)S(1)}, bf16[1024,256]{1,0:T(8,128)(2,1)S(1)}, u32[]{:S(2)}, u32[]{:S(2)}) collective-permute-start(bf16[1024,256]{1,0:T(8,128)(2,1)S(1)} %bitcast.24), channel_id=1, source_target_pairs={{0,32},{32,0},{64,96},{96,64},{128,160},{160,128},{192,224},{224,1... | collective-permute-start | bytes 1572872 | tf_op jit(solution)/shard_map/ppermute | solution.py:162
  155.1 12.0 %copy-start = (bf16[128,128]{1,0:T(8,128)(2,1)S(1)}, bf16[128,128]{1,0:T(8,128)(2,1)}, u32[]{:S(2)}) copy-start(bf16[128,128]{1,0:T(8,128)(2,1)} %param.10) | copy-start | bytes 98308
  155.1 28.6 %all-to-all-start.5 = ((bf16[32,32,256]{2,1,0:T(8,128)(2,1)}), bf16[32,32,256]{2,1,0:T(8,128)(2,1)S(1)}, u32[]{:S(2)}, u32[]{:S(2)}) async-start(bf16[32,32,256]{2,1,0:T(8,128)(2,1)} %bitcast.7), calls=%async_computation.5 | async-start | bytes 1048576 | tf_op jit(solution)/shard_map/all_to_all | solution.py:103

commit v2 on v0

v2 whole, which is shorter than its diff:
```python
import functools

import jax
import jax.numpy as jnp
from jax import lax
from jax.experimental import pallas as pl
from jax.experimental.pallas import tpu as pltpu
from jax.sharding import PartitionSpec as P

DIM = 128
BLOCK = 128
CAP = 16
LAYERS = 2
BOTH = 2 * DIM

SMEM = pl.BlockSpec(memory_space=pltpu.SMEM)
VMEM = pl.BlockSpec(memory_space=pltpu.VMEM)


def call(kernel, name, outs, ins, scratch=(), flops=0):
    return pl.pallas_call(
        kernel,
        out_shape=outs,
        in_specs=ins,
        out_specs=jax.tree.map(lambda _: VMEM, outs),
        scratch_shapes=scratch,
        cost_estimate=pl.CostEstimate(flops=flops, bytes_accessed=2**21, transcendentals=0),
        compiler_params=pltpu.CompilerParams(vmem_limit_bytes=24 * 2**20),
        name=name,
    )


def half(*shape):
    return jax.ShapeDtypeStruct(shape, jnp.bfloat16)


def single(*shape):
    return jax.ShapeDtypeStruct(shape, jnp.float32)


def add_views(acc_ref, block, keep_ref, s, prod):
    acc_ref[block, :, :DIM] += keep_ref[0, s] * prod[:, :DIM]
    acc_ref[block, :, DIM:] += keep_ref[1, s] * prod[:, -DIM:]


def host_kernel(
    rows_ref, slots_ref, keep_ref, w_ref, q_ref, own_ref, send_ref, acc_ref, *, lanes
):
    acc_ref[...] = jnp.zeros_like(acc_ref)
    owned = own_ref.shape[0]
    n = BLOCK // q_ref.shape[1]
    for s in range(CAP):
        q = q_ref[pl.ds(rows_ref[s] * n, n), :, -lanes:].reshape(BLOCK, lanes)
        prod = lax.dot_general(
            w_ref[s], q, (((0,), (0,)), ((), ())), preferred_element_type=jnp.float32
        )
        add_views(acc_ref, slots_ref[s], keep_ref, s, prod)
    own_ref[...] = acc_ref[:owned]
    send_ref[...] = acc_ref[owned:].astype(jnp.bfloat16)


def query_kernel(rows_ref, slots_ref, keep_ref, w_ref, mine_ref, other_ref, *refs):
    *extra, out_ref, acc_ref = refs
    acc_ref[...] = jnp.zeros_like(acc_ref)
    owned = mine_ref.shape[0]
    for s in range(CAP):
        slot = slots_ref[s]
        at = slot % owned
        host = jnp.where(slot < owned, mine_ref[at, :BLOCK], other_ref[at])
        prod = jnp.dot(w_ref[s], host, preferred_element_type=jnp.float32)
        add_views(acc_ref, rows_ref[s], keep_ref, s, prod)
    shape = out_ref.shape[:2]
    out_ref[:, :, :BOTH] = acc_ref[...].astype(jnp.bfloat16).reshape(shape + (BOTH,))
    if extra:
        out_ref[:, :, BOTH:] = jnp.broadcast_to(extra[0][...][None], shape + (DIM,))


def next_rows(scale_ref, total):
    now = (scale_ref[...] * total).astype(jnp.bfloat16)
    return now, (scale_ref[...] * now.astype(jnp.float32)).astype(jnp.bfloat16)


def query_update_kernel(in_ref, scale_ref, now_ref, copies_ref):
    total = jnp.sum(in_ref[:, :, :BOTH].astype(jnp.float32), axis=0)
    now, sent = next_rows(scale_ref, total)
    now_ref[...] = now
    copies_ref[...] = jnp.broadcast_to(sent[None], copies_ref.shape)


def host_update_kernel(in_ref, scale_ref, own_ref, other_ref, now_ref, out_ref):
    now, sent = next_rows(scale_ref, jnp.sum(in_ref[...].astype(jnp.float32), axis=0))
    now_ref[...] = now
    out_ref[:, :BLOCK] = jnp.broadcast_to(sent[None], in_ref.shape)
    pair = own_ref[...] + other_ref[...].astype(jnp.float32)
    out_ref[:, BLOCK:] = pair.astype(jnp.bfloat16)


def exchange(blocks, axis, groups=None):
    return lax.all_to_all(blocks, axis, 0, 0, axis_index_groups=groups, tiled=True)


def split_views(both):
    return jnp.stack([both[:, :DIM], both[:, DIM:]])


def per_device(
    query_embed,
    host_embed,
    query_degree,
    host_degree,
    tile_rows,
    tile_cols,
    tile_counts,
    keep_mask,
    live_tiles,
):
    n_pb, n_ha = lax.axis_size("pb"), lax.axis_size("ha")
    local = query_embed.shape[0]
    slab_blocks = n_ha * local // BLOCK
    chips = n_pb // 2
    core = lax.axis_index("pb") % 2
    same_core = [[2 * y + c for y in range(chips)] for c in range(2)]

    rows = tile_rows % slab_blocks
    cols = tile_cols // n_ha
    slots = ((cols % 2) ^ core) * chips + cols // 2
    live = jnp.arange(CAP, dtype=jnp.int32) < live_tiles[0]
    keep = (keep_mask * live[None]).astype(jnp.float32)
    weights = tile_counts.astype(jnp.bfloat16)
    scale_query = lax.rsqrt(query_degree.astype(jnp.float32))[:, None]
    scale_host = lax.rsqrt(host_degree.astype(jnp.float32))[:, None]

    def sent(scale, now):
        return (scale * now.astype(jnp.float32)).astype(jnp.bfloat16)

    def swap_core(blocks):
        return lax.ppermute(blocks, "pb", [(i, i ^ 1) for i in range(n_pb)])

    def host_sums(slab, lanes, blocks):
        return call(
            functools.partial(host_kernel, lanes=lanes),
            "host_sums",
            (single(chips, BLOCK, BOTH), half(chips, BLOCK, BOTH)),
            [SMEM, SMEM, SMEM, VMEM, VMEM],
            [pltpu.VMEM((n_pb, BLOCK, BOTH), jnp.float32)],
            2 * CAP * BLOCK * BLOCK * lanes,
        )(rows, blocks, keep, weights, slab)

    def query_sums(mine, other, *extra):
        lanes = mine.shape[2]
        return call(
            query_kernel,
            "query_sums",
            half(n_ha, local, BOTH + DIM * len(extra)),
            [SMEM, SMEM, SMEM] + [VMEM] * (3 + len(extra)),
            [pltpu.VMEM((slab_blocks, BLOCK, BOTH), jnp.float32)],
            2 * CAP * BLOCK * BLOCK * lanes,
        )(rows, slots, keep, weights, mine, other, *extra)

    sent_host = sent(scale_host, host_embed)
    mine = exchange(jnp.broadcast_to(sent_host[None], (chips, BLOCK, DIM)), "pb", same_core)

    arrived = exchange(query_sums(mine, swap_core(mine), sent(scale_query, query_embed)), "ha")
    query_1, copies = call(
        query_update_kernel,
        "query_update",
        (half(local, BOTH), half(n_ha, local, BOTH)),
        [VMEM] * 2,
    )(arrived, scale_query)

    slab = exchange(copies, "ha")
    own, send = host_sums(arrived, DIM, slots)
    pair = (own + swap_core(send).astype(jnp.float32)).astype(jnp.bfloat16)
    arrived = exchange(pair, "pb", same_core)

    own, send = host_sums(slab, BOTH, slots)
    host_1, chunks = call(
        host_update_kernel,
        "host_update",
        (half(BLOCK, BOTH), half(chips, 2 * BLOCK, BOTH)),
        [VMEM] * 4,
    )(arrived, scale_host, own, swap_core(send))
    arrived = exchange(chunks, "pb", same_core)
    host_2 = sent(scale_host, jnp.sum(arrived[:, BLOCK:].astype(jnp.float32), axis=0))

    arrived = exchange(query_sums(arrived, swap_core(arrived[:, :BLOCK])), "ha")
    query_2 = sent(scale_query, jnp.sum(arrived.astype(jnp.float32), axis=0))

    def mean(embed, one, two):
        zero = embed.astype(jnp.float32)[None]
        total = zero + split_views(one).astype(jnp.float32) + split_views(two).astype(jnp.float32)
        return (total / (LAYERS + 1)).astype(jnp.bfloat16)

    return (mean(query_embed, query_1, query_2), mean(host_embed, host_1, host_2))


def solution(mesh):
    in_specs = (
        P(("pb", "ha"), None),
        P(("pb", "ha"), None),
        P(("pb", "ha")),
        P(("pb", "ha")),
        P(("pb", "ha")),
        P(("pb", "ha")),
        P(("pb", "ha"), None, None),
        P(None, ("pb", "ha")),
        P(("pb", "ha")),
    )
    out_specs = (P(None, ("pb", "ha"), None), P(None, ("pb", "ha"), None))
    return jax.shard_map(
        per_device, mesh=mesh, in_specs=in_specs, out_specs=out_specs, check_vma=False
    )
```

time: 787 us -> 169 us (0.21)
  waiting for transfers between devices: 652 us -> 62.8 us
  starting transfers between devices: 0.43 us -> 62 us
  blocking collectives: 71.6 us -> 26.1 us
  other arithmetic: 25.9 us -> 5.5 us
  between operations: 15 us -> 1.53 us
  local copies, waits for them, and re-layouts: 13.2 us -> 2.32 us
    reduce_scatter x4 -> x0, waiting for transfers between devices: 564 us -> none  [the longest x2 426 us: regroup(): lax.psum_scatter(query_part.astype(jnp.bfloat16), 'ha', scatter_dimension...]
    all_gather x2 -> x0, waiting for transfers between devices: 88.2 us -> none  [collect(): host_group = lax.all_gather(sent_host, 'pb', axis=1, tiled=True)]
    all_gather x2 -> x0, blocking collectives: 71.6 us -> none  [collect(): query_slab = lax.all_gather(sent_query, 'ha', axis=1, tiled=True)]
    all_to_all x0 -> x5, waiting for transfers between devices: none -> 59.8 us  [exchange(): lax.all_to_all(blocks, axis, 0, 0, axis_index_groups=groups, tiled=True)]
    all_to_all x0 -> x5, starting transfers between devices: none -> 39.4 us  [exchange(): lax.all_to_all(blocks, axis, 0, 0, axis_index_groups=groups, tiled=True)]
    all_to_all x0 -> x1, blocking collectives: none -> 26.1 us  [exchange(): lax.all_to_all(blocks, axis, 0, 0, axis_index_groups=groups, tiled=True)]
    ppermute x0 -> x4, starting transfers between devices: none -> 22.7 us  [swap_core(): return lax.ppermute(blocks, 'pb', [(i, i ^ 1) for i in range(n_pb)])]
    scatter-add x4 -> x0, other arithmetic: 13.2 us -> none  [the longest x2 7.32 us: tile_terms(): jnp.zeros(host_blocks.shape, jnp.float32).at[:, block_col].add(host_prod)]
  transfers between devices with their start and end apart: 6 -> 9, of which waited for: 6 -> 7; matrix products, arithmetic and copies ran while one was open for 1% -> 2% of each run, Pallas kernels for 0% -> 1%
where the time goes in v2:
time: 169 us; the launch traced here: 168 us
  waiting for transfers between devices  62.8 us (37%)
  starting transfers between devices  62 us (37%)
  blocking collectives  26.1 us (15%)
  Pallas kernels  7.48 us (4%)
  other arithmetic  5.5 us (3%)
  local copies, waits for them, and re-layouts  2.32 us (1%)
    all_to_all x5, waiting for transfers between devices, exchange(): lax.all_to_all(blocks, axis, 0, 0, axis_index_groups=groups, tiled=True)  59.8 us
    all_to_all x5, starting transfers between devices, exchange(): lax.all_to_all(blocks, axis, 0, 0, axis_index_groups=groups, tiled=True)  39.4 us
    all_to_all x1, blocking collectives, exchange(): lax.all_to_all(blocks, axis, 0, 0, axis_index_groups=groups, tiled=True)  26.1 us
    ppermute x4, starting transfers between devices, swap_core(): return lax.ppermute(blocks, 'pb', [(i, i ^ 1) for i in range(n_pb)])  22.7 us
    pallas_call x2, Pallas kernels, query_sums(): call(query_kernel, 'query_sums', half(n_ha, local, BOTH + DIM * len(extra...  3.87 us
  transfers between devices with their start and end apart: 9, of which 7 were waited for; matrix products, arithmetic and copies ran while one was open for 2% of the time, Pallas kernels for 1%

profile of v2, /device:TPU:1, one launch (start us, length us, event | category | flops | bytes accessed | tf_op | source)
XLA Modules:
  0.0 167.7 jit_solution(16493975801079089569)
XLA Ops:
  0.6 0.7 fusion.4
  1.3 0.8 multiply_convert_fusion.2
  2.1 0.7 broadcast_in_dim.6
  2.9 7.7 %all-to-all-start = ((bf16[8,128,128]{2,1,0:T(8,128)(2,1)}), bf16[8,128,128]{2,1,0:T(8,128)(2,1)S(1)}, u32[]{:S(2)}, u32[]{:S(2)}) async-start(bf16[8,128,128]{2,1,0:T(8,128)(2,1)} %broadcast_in_dim.6), calls=%async_computation | async-start | bytes 524288 | tf_op jit(solution)/shard_map/all_to_all | solution.py:99
  11.2 0.6 copy-done.3
  11.9 0.7 copy-done.2
  12.6 7.4 %all-to-all-done.mine_ref = bf16[8,128,128]{2,1,0:T(8,128)(2,1)S(1)} async-done(((bf16[8,128,128]{2,1,0:T(8,128)(2,1)}), bf16[8,128,128]{2,1,0:T(8,128)(2,1)S(1)}, u32[]{:S(2)}, u32[]{:S(2)}) %all-to-all-start) | async-done | bytes 262176 | tf_op jit(solution)/shard_map/all_to_all | solution.py:99
  19.9 5.5 %collective-permute-start = (bf16[8,128,128]{2,1,0:T(8,128)(2,1)S(1)}, bf16[8,128,128]{2,1,0:T(8,128)(2,1)S(1)}, u32[]{:S(2)}, u32[]{:S(2)}) collective-permute-start(bf16[8,128,128]{2,1,0:T(8,128)(2,1)S(1)} %all-to-all-done.mine_ref), channel_id=1, source_target_pairs={{0,32},{32,0},{64,96},{96,64},{128,160},{160,128},{192,224},{224,1... | collective-permute-start | bytes 786440 | tf_op jit(solution)/shard_map/ppermute | solution.py:137
  25.5 1.3 convert_element_type.73.w_ref
  26.9 2.0 %query_sums.2 = bf16[32,32,384]{2,1,0:T(8,128)(2,1)} custom-call(s32[16]{0:T(128)S(1)} %get-tuple-element.30.rows_ref, s32[16]{0:T(128)S(1)} %get-tuple-element.31.slots_ref, f32[2,16]{1,0:T(2,128)S(1)} %multiply_convert_fusion.6.keep_ref, bf16[16,128,128]{2,1,0:T(8,128)(2,1)S(1)} %convert_element_type.73.w_ref, ...), custom_call_target="tpu_custom_call" | custom-call | flops 67108864 | bytes 2097152 | tf_op jit(solution)/shard_map/query_sums/pallas_call | solution.py:151
  28.9 12.7 %all-to-all-start.1 = ((bf16[32,32,384]{2,1,0:T(8,128)(2,1)}), bf16[32,32,384]{2,1,0:T(8,128)(2,1)S(1)}, u32[]{:S(2)}, u32[]{:S(2)}) async-start(bf16[32,32,384]{2,1,0:T(8,128)(2,1)} %query_sums.2), calls=%async_computation.1 | async-start | bytes 1572864 | tf_op jit(solution)/shard_map/all_to_all | solution.py:99
  41.7 21.7 %all-to-all-done.1.in_ref.q_ref = bf16[32,32,384]{2,1,0:T(8,128)(2,1)S(1)} async-done(((bf16[32,32,384]{2,1,0:T(8,128)(2,1)}), bf16[32,32,384]{2,1,0:T(8,128)(2,1)S(1)}, u32[]{:S(2)}, u32[]{:S(2)}) %all-to-all-start.1) | async-done | bytes 786464 | tf_op jit(solution)/shard_map/all_to_all | solution.py:99
  63.4 0.9 query_update.1
  64.3 5.4 %all-to-all-start.3 = ((bf16[32,32,256]{2,1,0:T(8,128)(2,1)}), bf16[32,32,256]{2,1,0:T(8,128)(2,1)S(1)}, u32[]{:S(2)}, u32[]{:S(2)}) async-start(bf16[32,32,256]{2,1,0:T(8,128)(2,1)} %get-tuple-element.13), calls=%async_computation.3 | async-start | bytes 1048576 | tf_op jit(solution)/shard_map/all_to_all | solution.py:99
  69.7 1.2 host_sums.2
  70.9 3.7 %collective-permute-start.1 = (bf16[8,128,256]{2,1,0:T(8,128)(2,1)S(1)}, bf16[8,128,256]{2,1,0:T(8,128)(2,1)S(1)}, u32[]{:S(2)}, u32[]{:S(2)}) collective-permute-start(bf16[8,128,256]{2,1,0:T(8,128)(2,1)S(1)} %get-tuple-element.12), channel_id=1, source_target_pairs={{0,32},{32,0},{64,96},{96,64},{128,160},{160,128},{192,224},{224,1... | collective-permute-start | bytes 1572872 | tf_op jit(solution)/shard_map/ppermute | solution.py:137
  74.6 1.5 collective-permute-done.1
  76.1 1.0 add_convert_fusion
  77.1 7.9 %all-to-all-done.3.q_ref = bf16[32,32,256]{2,1,0:T(8,128)(2,1)S(1)} async-done(((bf16[32,32,256]{2,1,0:T(8,128)(2,1)}), bf16[32,32,256]{2,1,0:T(8,128)(2,1)S(1)}, u32[]{:S(2)}, u32[]{:S(2)}) %all-to-all-start.3) | async-done | bytes 524320 | tf_op jit(solution)/shard_map/all_to_all | solution.py:99
  85.0 3.5 %all-to-all-start.2 = ((bf16[8,128,256]{2,1,0:T(8,128)(2,1)}), bf16[8,128,256]{2,1,0:T(8,128)(2,1)S(1)}, u32[]{:S(2)}, u32[]{:S(2)}) async-start(bf16[8,128,256]{2,1,0:T(8,128)(2,1)} %add_convert_fusion), calls=%async_computation.2 | async-start | bytes 1048576 | tf_op jit(solution)/shard_map/all_to_all | solution.py:99
  88.5 1.2 host_sums.3
  89.7 5.5 %collective-permute-start.2 = (bf16[8,128,256]{2,1,0:T(8,128)(2,1)S(1)}, bf16[8,128,256]{2,1,0:T(8,128)(2,1)S(1)}, u32[]{:S(2)}, u32[]{:S(2)}) collective-permute-start(bf16[8,128,256]{2,1,0:T(8,128)(2,1)S(1)} %get-tuple-element.15), channel_id=1, source_target_pairs={{0,32},{32,0},{64,96},{96,64},{128,160},{160,128},{192,224},{224,1... | collective-permute-start | bytes 1572872 | tf_op jit(solution)/shard_map/ppermute | solution.py:137
  95.3 7.1 %all-to-all-done.2.in_ref = bf16[8,128,256]{2,1,0:T(8,128)(2,1)S(1)} async-done(((bf16[8,128,256]{2,1,0:T(8,128)(2,1)}), bf16[8,128,256]{2,1,0:T(8,128)(2,1)S(1)}, u32[]{:S(2)}, u32[]{:S(2)}) %all-to-all-start.2) | async-done | bytes 524320 | tf_op jit(solution)/shard_map/all_to_all | solution.py:99
  102.5 0.3 host_update.1
  102.7 26.1 %all_to_all.30.mine_ref = bf16[8,256,256]{2,1,0:T(8,128)(2,1)S(1)} all-to-all(bf16[8,256,256]{2,1,0:T(8,128)(2,1)S(1)} %get-tuple-element.16), channel_id=1, replica_groups={{0,64,128,192,256,320,384,448},{32,96,160,224,288,352,416,480},{1,65,12..., dimensions={0} | all-to-all | bytes 2097152 | tf_op jit(solution)/shard_map/all_to_all | solution.py:99
  128.8 8.0 %collective-permute-start.3 = (bf16[8,128,256]{2,1,0:T(8,128)(2,1)S(1)}, bf16[8,128,256]{2,1,0:T(8,128)(2,1)S(1)}, u32[]{:S(2)}, u32[]{:S(2)}) collective-permute-start(bf16[8,128,256]{2,1,0:T(8,128)(2,1)S(1)} %slice.40), channel_id=1, source_target_pairs={{0,32},{32,0},{64,96},{96,64},{128,160},{160,128},{192,224},{224,1... | collective-permute-start | bytes 1572872 | tf_op jit(solution)/shard_map/ppermute | solution.py:137
  136.9 1.5 collective-permute-done.3.other_ref
  138.3 1.9 %query_sums.3 = bf16[32,32,256]{2,1,0:T(8,128)(2,1)} custom-call(s32[16]{0:T(128)S(1)} %get-tuple-element.30.rows_ref, s32[16]{0:T(128)S(1)} %get-tuple-element.31.slots_ref, f32[2,16]{1,0:T(2,128)S(1)} %multiply_convert_fusion.6.keep_ref, bf16[16,128,128]{2,1,0:T(8,128)(2,1)S(1)} %convert_element_type.73.w_ref, ...), custom_call_target="tpu_custom_call" | custom-call | flops 134217728 | bytes 2097152 | tf_op jit(solution)/shard_map/query_sums/pallas_call | solution.py:151
  140.2 10.1 %all-to-all-start.5 = ((bf16[32,32,256]{2,1,0:T(8,128)(2,1)}), bf16[32,32,256]{2,1,0:T(8,128)(2,1)S(1)}, u32[]{:S(2)}, u32[]{:S(2)}) async-start(bf16[32,32,256]{2,1,0:T(8,128)(2,1)} %query_sums.3), calls=%async_computation.5 | async-start | bytes 1048576 | tf_op jit(solution)/shard_map/all_to_all | solution.py:99
  150.5 0.7 multiply_convert_fusion
  151.2 15.7 %all-to-all-done.5 = bf16[32,32,256]{2,1,0:T(8,128)(2,1)S(1)} async-done(((bf16[32,32,256]{2,1,0:T(8,128)(2,1)}), bf16[32,32,256]{2,1,0:T(8,128)(2,1)S(1)}, u32[]{:S(2)}, u32[]{:S(2)}) %all-to-all-start.5) | async-done | bytes 524320 | tf_op jit(solution)/shard_map/all_to_all | solution.py:99
  167.1 0.6 multiply_convert_fusion.3
  (30 shorter events, 0.7 us)
Async XLA Ops:
  2.9 17.1 %all-to-all-start = ((bf16[8,128,128]{2,1,0:T(8,128)(2,1)}), bf16[8,128,128]{2,1,0:T(8,128)(2,1)S(1)}, u32[]{:S(2)}, u32[]{:S(2)}) async-start(bf16[8,128,128]{2,1,0:T(8,128)(2,1)} %broadcast_in_dim.6), calls=%async_computation | async-start | bytes 524288 | tf_op jit(solution)/shard_map/all_to_all | solution.py:99
  11.2 0.7 copy-start.3
  11.2 0.7 copy-start.4
  11.9 0.7 copy-start.2
  12.5 12.9 %copy-start.5 = (s32[32]{0:T(128)S(1)}, s32[32]{0:T(128)}, u32[]{:S(2)}) copy-start(s32[32]{0:T(128)} %param.11) | copy-start | bytes 388
  19.9 7.0 %collective-permute-start = (bf16[8,128,128]{2,1,0:T(8,128)(2,1)S(1)}, bf16[8,128,128]{2,1,0:T(8,128)(2,1)S(1)}, u32[]{:S(2)}, u32[]{:S(2)}) collective-permute-start(bf16[8,128,128]{2,1,0:T(8,128)(2,1)S(1)} %all-to-all-done.mine_ref), channel_id=1, source_target_pairs={{0,32},{32,0},{64,96},{96,64},{128,160},{160,128},{192,224},{224,1... | collective-permute-start | bytes 786440 | tf_op jit(solution)/shard_map/ppermute | solution.py:137
  25.5 1.4 copy-start.1
  28.9 34.5 %all-to-all-start.1 = ((bf16[32,32,384]{2,1,0:T(8,128)(2,1)}), bf16[32,32,384]{2,1,0:T(8,128)(2,1)S(1)}, u32[]{:S(2)}, u32[]{:S(2)}) async-start(bf16[32,32,384]{2,1,0:T(8,128)(2,1)} %query_sums.2), calls=%async_computation.1 | async-start | bytes 1572864 | tf_op jit(solution)/shard_map/all_to_all | solution.py:99
  64.3 20.7 %all-to-all-start.3 = ((bf16[32,32,256]{2,1,0:T(8,128)(2,1)}), bf16[32,32,256]{2,1,0:T(8,128)(2,1)S(1)}, u32[]{:S(2)}, u32[]{:S(2)}) async-start(bf16[32,32,256]{2,1,0:T(8,128)(2,1)} %get-tuple-element.13), calls=%async_computation.3 | async-start | bytes 1048576 | tf_op jit(solution)/shard_map/all_to_all | solution.py:99
  70.9 5.2 %collective-permute-start.1 = (bf16[8,128,256]{2,1,0:T(8,128)(2,1)S(1)}, bf16[8,128,256]{2,1,0:T(8,128)(2,1)S(1)}, u32[]{:S(2)}, u32[]{:S(2)}) collective-permute-start(bf16[8,128,256]{2,1,0:T(8,128)(2,1)S(1)} %get-tuple-element.12), channel_id=1, source_target_pairs={{0,32},{32,0},{64,96},{96,64},{128,160},{160,128},{192,224},{224,1... | collective-permute-start | bytes 1572872 | tf_op jit(solution)/shard_map/ppermute | solution.py:137
  85.0 17.5 %all-to-all-start.2 = ((bf16[8,128,256]{2,1,0:T(8,128)(2,1)}), bf16[8,128,256]{2,1,0:T(8,128)(2,1)S(1)}, u32[]{:S(2)}, u32[]{:S(2)}) async-start(bf16[8,128,256]{2,1,0:T(8,128)(2,1)} %add_convert_fusion), calls=%async_computation.2 | async-start | bytes 1048576 | tf_op jit(solution)/shard_map/all_to_all | solution.py:99
  89.7 12.8 %collective-permute-start.2 = (bf16[8,128,256]{2,1,0:T(8,128)(2,1)S(1)}, bf16[8,128,256]{2,1,0:T(8,128)(2,1)S(1)}, u32[]{:S(2)}, u32[]{:S(2)}) collective-permute-start(bf16[8,128,256]{2,1,0:T(8,128)(2,1)S(1)} %get-tuple-element.15), channel_id=1, source_target_pairs={{0,32},{32,0},{64,96},{96,64},{128,160},{160,128},{192,224},{224,1... | collective-permute-start | bytes 1572872 | tf_op jit(solution)/shard_map/ppermute | solution.py:137
  128.8 8.0 %copy-start = (bf16[128,128]{1,0:T(8,128)(2,1)S(1)}, bf16[128,128]{1,0:T(8,128)(2,1)}, u32[]{:S(2)}) copy-start(bf16[128,128]{1,0:T(8,128)(2,1)} %param.10) | copy-start | bytes 98308
  128.8 9.5 %collective-permute-start.3 = (bf16[8,128,256]{2,1,0:T(8,128)(2,1)S(1)}, bf16[8,128,256]{2,1,0:T(8,128)(2,1)S(1)}, u32[]{:S(2)}, u32[]{:S(2)}) collective-permute-start(bf16[8,128,256]{2,1,0:T(8,128)(2,1)S(1)} %slice.40), channel_id=1, source_target_pairs={{0,32},{32,0},{64,96},{96,64},{128,160},{160,128},{192,224},{224,1... | collective-permute-start | bytes 1572872 | tf_op jit(solution)/shard_map/ppermute | solution.py:137
  140.2 26.7 %all-to-all-start.5 = ((bf16[32,32,256]{2,1,0:T(8,128)(2,1)}), bf16[32,32,256]{2,1,0:T(8,128)(2,1)S(1)}, u32[]{:S(2)}, u32[]{:S(2)}) async-start(bf16[32,32,256]{2,1,0:T(8,128)(2,1)} %query_sums.3), calls=%async_computation.5 | async-start | bytes 1048576 | tf_op jit(solution)/shard_map/all_to_all | solution.py:99

commit v3 on v2

v3 whole, which is shorter than its diff:
```python
import jax
import jax.numpy as jnp
from jax import lax
from jax.experimental import pallas as pl
from jax.experimental.pallas import tpu as pltpu
from jax.sharding import PartitionSpec as P

DIM = 128
BLOCK = 128
CAP = 16
LAYERS = 2
BOTH = 2 * DIM

ANY = pl.BlockSpec(memory_space=pl.ANY)
SMEM = pl.BlockSpec(memory_space=pltpu.SMEM)
VMEM = pl.BlockSpec(memory_space=pltpu.VMEM)


def call(kernel, name, outs, ins, scratch=(), flops=0):
    return pl.pallas_call(
        kernel,
        out_shape=outs,
        in_specs=ins,
        out_specs=jax.tree.map(lambda _: VMEM, outs),
        scratch_shapes=scratch,
        cost_estimate=pl.CostEstimate(flops=flops, bytes_accessed=2**21, transcendentals=0),
        compiler_params=pltpu.CompilerParams(vmem_limit_bytes=24 * 2**20),
        name=name,
    )


def half(*shape):
    return jax.ShapeDtypeStruct(shape, jnp.bfloat16)


def single(*shape):
    return jax.ShapeDtypeStruct(shape, jnp.float32)


def add_views(acc_ref, block, keep_ref, s, prod):
    acc_ref[block, :, :DIM] += keep_ref[0, s] * prod[:, :DIM]
    acc_ref[block, :, DIM:] += keep_ref[1, s] * prod[:, -DIM:]


def host_kernel(
    rows_ref, slots_ref, keep_ref, w_ref, q_ref, after_ref, own_ref, send_ref, acc_ref
):
    del after_ref
    acc_ref[...] = jnp.zeros_like(acc_ref)
    owned = own_ref.shape[0]
    n = BLOCK // q_ref.shape[1]
    for s in range(CAP):
        q = q_ref[pl.ds(rows_ref[s] * n, n)].reshape(BLOCK, q_ref.shape[2])
        prod = lax.dot_general(
            w_ref[s], q, (((0,), (0,)), ((), ())), preferred_element_type=jnp.float32
        )
        add_views(acc_ref, slots_ref[s], keep_ref, s, prod)
    own_ref[...] = acc_ref[:owned]
    send_ref[...] = acc_ref[owned:].astype(jnp.bfloat16)


def query_kernel(
    rows_ref, slots_ref, keep_ref, w_ref, mine_ref, other_ref, after_ref, out_ref, acc_ref
):
    del after_ref
    acc_ref[...] = jnp.zeros_like(acc_ref)
    owned = mine_ref.shape[0]
    for s in range(CAP):
        slot = slots_ref[s]
        at = slot % owned
        host = jnp.where(slot < owned, mine_ref[at], other_ref[at])
        prod = jnp.dot(w_ref[s], host, preferred_element_type=jnp.float32)
        add_views(acc_ref, rows_ref[s], keep_ref, s, prod)
    out_ref[...] = acc_ref[...].astype(jnp.bfloat16).reshape(out_ref.shape)


def next_rows(scale_ref, total):
    now = (scale_ref[...] * total).astype(jnp.bfloat16)
    return now, (scale_ref[...] * now.astype(jnp.float32)).astype(jnp.bfloat16)


def update_kernel(in_ref, scale_ref, after_ref, now_ref, copies_ref):
    del after_ref
    now, sent = next_rows(scale_ref, jnp.sum(in_ref[...].astype(jnp.float32), axis=0))
    now_ref[...] = now
    copies_ref[...] = jnp.broadcast_to(sent[None], copies_ref.shape)


def spread_kernel(scale_ref, embed_ref, after_ref, out_ref):
    del after_ref
    sent = (scale_ref[...] * embed_ref[...].astype(jnp.float32)).astype(jnp.bfloat16)
    out_ref[...] = jnp.broadcast_to(sent[None], out_ref.shape)


def cast_kernel(total_ref, after_ref, *out_refs):
    del after_ref
    for index, out_ref in enumerate(out_refs, 1):
        out_ref[...] = total_ref[index].astype(jnp.bfloat16)


def exchange(blocks, axis, groups=None):
    return lax.all_to_all(blocks, axis, 0, 0, axis_index_groups=groups, tiled=True)


def reverse_bits(index, bits):
    return sum(((index >> b) & 1) << (bits - 1 - b) for b in range(bits))


def split_views(both):
    return jnp.stack([both[:, :DIM], both[:, DIM:]])


def per_device(
    query_embed,
    host_embed,
    query_degree,
    host_degree,
    tile_rows,
    tile_cols,
    tile_counts,
    keep_mask,
    live_tiles,
):
    n_pb, n_ha = lax.axis_size("pb"), lax.axis_size("ha")
    local = query_embed.shape[0]
    slab_blocks = n_ha * local // BLOCK
    chips = n_pb // 2
    core = lax.axis_index("pb") % 2
    same_core = [[2 * y + c for y in range(chips)] for c in range(2)]

    rows = tile_rows % slab_blocks
    cols = tile_cols // n_ha
    slots = ((cols % 2) ^ core) * chips + cols // 2
    bits = n_pb.bit_length() - 1
    by_bits = reverse_bits(cols ^ lax.axis_index("pb"), bits)
    live = jnp.arange(CAP, dtype=jnp.int32) < live_tiles[0]
    keep = (keep_mask * live[None]).astype(jnp.float32)
    weights = tile_counts.astype(jnp.bfloat16)
    scale_query = lax.rsqrt(query_degree.astype(jnp.float32))[:, None]
    scale_host = lax.rsqrt(host_degree.astype(jnp.float32))[:, None]

    def sent(scale, now):
        return (scale * now.astype(jnp.float32)).astype(jnp.bfloat16)

    def swap(blocks, axis, bit):
        size = lax.axis_size(axis)
        return lax.ppermute(blocks, axis, [(i, i ^ (1 << bit)) for i in range(size)])

    def swap_core(blocks):
        return swap(blocks, "pb", 0)

    def host_sums(slab, after):
        return call(
            host_kernel,
            "host_sums",
            (single(chips, BLOCK, BOTH), half(chips, BLOCK, BOTH)),
            [SMEM, SMEM, SMEM, VMEM, VMEM, ANY],
            [pltpu.VMEM((n_pb, BLOCK, BOTH), jnp.float32)],
            2 * CAP * BLOCK * BLOCK * slab.shape[2],
        )(rows, by_bits, keep, weights, slab, after)

    def query_sums(mine, slots, after):
        return call(
            query_kernel,
            "query_sums",
            half(n_ha, local, BOTH),
            [SMEM, SMEM, SMEM, VMEM, VMEM, VMEM, ANY],
            [pltpu.VMEM((slab_blocks, BLOCK, BOTH), jnp.float32)],
            2 * CAP * BLOCK * BLOCK * mine.shape[2],
        )(rows, slots, keep, weights, mine, swap_core(mine), after)

    def gather_steps(block):
        steps = [block[None]]
        for bit in range(bits - 1, 0, -1):
            steps.append(jnp.concatenate([steps[-1], swap(steps[-1], "pb", bit)]))
        return steps

    def reduce_steps(own, send):
        steps = [own + swap_core(send).astype(jnp.float32)]
        for bit in range(1, bits):
            total = steps[-1]
            size = total.shape[0] // 2
            other = swap(total[size:].astype(jnp.bfloat16), "pb", bit)
            steps.append(total[:size] + other.astype(jnp.float32))
        return steps

    def update(name, arrived, scale, copies, after):
        shape = arrived.shape[1:]
        return call(
            update_kernel, name, (half(*shape), half(copies, *shape)), [VMEM, VMEM, ANY]
        )(arrived, scale, after)

    def spread(name, scale, embed, copies, after):
        return call(spread_kernel, name, half(copies, *embed.shape), [VMEM, VMEM, ANY])(
            scale, embed, after
        )

    mine = exchange(spread("host_spread", scale_host, host_embed, chips, query_embed), "pb", same_core)
    slab = exchange(spread("query_spread", scale_query, query_embed, n_ha, mine), "ha")
    part = query_sums(mine, slots, mine)
    arrived = exchange(part, "ha")
    sums_0 = reduce_steps(*host_sums(slab, part))
    query_1, copies = update("query_update", arrived, scale_query, n_ha, sums_0[0])

    slab = exchange(copies, "ha")
    host_1, copies = update("host_update", sums_0[-1], scale_host, chips, slab)
    mine = exchange(copies, "pb", same_core)
    own, send = host_sums(slab, copies)
    total = own + swap_core(send).astype(jnp.float32)
    size = total.shape[0] // 2
    total = total[:size] + swap(total[size:].astype(jnp.bfloat16), "pb", 1).astype(jnp.float32)
    part = query_sums(mine, slots, mine)
    arrived = exchange(part, "ha")
    blocks = call(cast_kernel, "cast", (half(BLOCK, BOTH),) * (size - 1), [VMEM, ANY])(total, part)
    host_sum = total[0]
    for index, block in enumerate(blocks, 1):
        away = reverse_bits(index, bits - 2) << 2
        other = lax.ppermute(block, "pb", [(i, i ^ away) for i in range(n_pb)])
        host_sum = host_sum + other.astype(jnp.float32)
    host_2 = sent(scale_host, host_sum)
    query_2 = sent(scale_query, jnp.sum(arrived.astype(jnp.float32), axis=0))

    def mean(embed, one, two):
        zero = embed.astype(jnp.float32)[None]
        total = zero + split_views(one).astype(jnp.float32) + split_views(two).astype(jnp.float32)
        return (total / (LAYERS + 1)).astype(jnp.bfloat16)

    return (mean(query_embed, query_1, query_2), mean(host_embed, host_1, host_2))


def solution(mesh):
    in_specs = (
        P(("pb", "ha"), None),
        P(("pb", "ha"), None),
        P(("pb", "ha")),
        P(("pb", "ha")),
        P(("pb", "ha")),
        P(("pb", "ha")),
        P(("pb", "ha"), None, None),
        P(None, ("pb", "ha")),
        P(("pb", "ha")),
    )
    out_specs = (P(None, ("pb", "ha"), None), P(None, ("pb", "ha"), None))
    return jax.shard_map(
        per_device, mesh=mesh, in_specs=in_specs, out_specs=out_specs, check_vma=False
    )
```

time: 169 us -> 153 us (0.905)
  blocking collectives: 26.1 us -> 0 us
  starting transfers between devices: 62 us -> 81.8 us
  waiting for transfers between devices: 62.8 us -> 51.6 us
  Pallas kernels: 7.48 us -> 10.4 us
    all_to_all x5 -> x6, waiting for transfers between devices: 59.8 us -> 28.3 us  [exchange(): lax.all_to_all(blocks, axis, 0, 0, axis_index_groups=groups, tiled=True)]
    all_to_all x1 -> x0, blocking collectives: 26.1 us -> none  [exchange(): lax.all_to_all(blocks, axis, 0, 0, axis_index_groups=groups, tiled=True)]
    ppermute x4 -> x11, waiting for transfers between devices: 2.99 us -> 23.2 us  [the longest x8 17.7 us: swap(): return lax.ppermute(blocks, axis, [(i, i ^ 1 << bit) for i in range(size)])]
    ppermute x4 -> x11, starting transfers between devices: 22.7 us -> 35.2 us  [the longest x8 23.8 us: swap(): return lax.ppermute(blocks, axis, [(i, i ^ 1 << bit) for i in range(size)])]
    all_to_all x5 -> x6, starting transfers between devices: 39.4 us -> 46.6 us  [exchange(): lax.all_to_all(blocks, axis, 0, 0, axis_index_groups=groups, tiled=True)]
    pallas_call x6 -> x9, Pallas kernels: 7.48 us -> 10.4 us  [the longest x2 3.76 us: query_sums(): call(query_kernel, 'query_sums', half(n_ha, local, BOTH), [SMEM, SMEM, SM...]
  transfers between devices with their start and end apart: 9 -> 17, of which waited for: 7 -> 9; matrix products, arithmetic and copies ran while one was open for 2% -> 2% of each run, Pallas kernels for 1% -> 5%
where the time goes in v3:
time: 153 us; the launch traced here: 152 us
  starting transfers between devices  81.8 us (53%)
  waiting for transfers between devices  51.6 us (34%)
  Pallas kernels  10.4 us (7%)
  other arithmetic  4.04 us (3%)
  local copies, waits for them, and re-layouts  2.18 us (1%)
  between operations  1.67 us (1%)
    all_to_all x6, starting transfers between devices, exchange(): lax.all_to_all(blocks, axis, 0, 0, axis_index_groups=groups, tiled=True)  46.6 us
    all_to_all x6, waiting for transfers between devices, exchange(): lax.all_to_all(blocks, axis, 0, 0, axis_index_groups=groups, tiled=True)  28.3 us
    ppermute x8, starting transfers between devices, swap(): return lax.ppermute(blocks, axis, [(i, i ^ 1 << bit) for i in range(size)])  23.8 us
    ppermute x8, waiting for transfers between devices, swap(): return lax.ppermute(blocks, axis, [(i, i ^ 1 << bit) for i in range(size)])  17.7 us
    ppermute x3, starting transfers between devices, per_device(): other = lax.ppermute(block, 'pb', [(i, i ^ away) for i in range(n_pb)])  11.4 us
    ppermute x3, waiting for transfers between devices, per_device(): other = lax.ppermute(block, 'pb', [(i, i ^ away) for i in range(n_pb)])  5.5 us
    pallas_call x2, Pallas kernels, query_sums(): call(query_kernel, 'query_sums', half(n_ha, local, BOTH), [SMEM, SMEM, SM...  3.76 us
    pallas_call x2, Pallas kernels, host_sums(): call(host_kernel, 'host_sums', (single(chips, BLOCK, BOTH), half(chips, B...  3.21 us
  transfers between devices with their start and end apart: 17, of which 9 were waited for; matrix products, arithmetic and copies ran while one was open for 2% of the time, Pallas kernels for 5%

profile of v3, /device:TPU:1, one launch (start us, length us, event | category | flops | bytes accessed | tf_op | source)
XLA Modules:
  0.0 151.7 jit_solution(9953271706939529106)
XLA Ops:
  2.9 7.7 %all-to-all-start = ((bf16[8,128,128]{2,1,0:T(8,128)(2,1)}), bf16[8,128,128]{2,1,0:T(8,128)(2,1)S(1)}, u32[]{:S(2)}, u32[]{:S(2)}) async-start(bf16[8,128,128]{2,1,0:T(8,128)(2,1)} %host_spread.1), calls=%async_computation | async-start | bytes 524288 | tf_op jit(solution)/shard_map/all_to_all | solution.py:102
  12.6 7.3 %all-to-all-done.mine_ref.after_ref = bf16[8,128,128]{2,1,0:T(8,128)(2,1)S(1)} async-done(((bf16[8,128,128]{2,1,0:T(8,128)(2,1)}), bf16[8,128,128]{2,1,0:T(8,128)(2,1)S(1)}, u32[]{:S(2)}, u32[]{:S(2)}) %all-to-all-start) | async-done | bytes 262176 | tf_op jit(solution)/shard_map/all_to_all | solution.py:102
  19.9 0.8 query_spread.1
  20.7 13.8 %all-to-all-start.2 = ((bf16[32,32,128]{2,1,0:T(8,128)(2,1)}), bf16[32,32,128]{2,1,0:T(8,128)(2,1)S(1)}, u32[]{:S(2)}, u32[]{:S(2)}) async-start(bf16[32,32,128]{2,1,0:T(8,128)(2,1)} %query_spread.1), calls=%async_computation.2 | async-start | bytes 524288 | tf_op jit(solution)/shard_map/all_to_all | solution.py:102
  35.2 4.7 %collective-permute-start = (bf16[8,128,128]{2,1,0:T(8,128)(2,1)S(1)}, bf16[8,128,128]{2,1,0:T(8,128)(2,1)S(1)}, u32[]{:S(2)}, u32[]{:S(2)}) collective-permute-start(bf16[8,128,128]{2,1,0:T(8,128)(2,1)S(1)} %all-to-all-done.mine_ref.after_ref), channel_id=1, source_target_pairs={{0,32},{32,0},{64,96},{96,64},{128,160},{160,128},{192,224},{224,1... | collective-permute-start | bytes 786440 | tf_op jit(solution)/shard_map/ppermute | solution.py:147
  41.0 1.9 %query_sums.2.after_ref = bf16[32,32,256]{2,1,0:T(8,128)(2,1)} custom-call(s32[16]{0:T(128)S(1)} %get-tuple-element.38.rows_ref, s32[16]{0:T(128)S(1)} %get-tuple-element.39.slots_ref, f32[2,16]{1,0:T(2,128)S(1)} %multiply_convert_fusion.3.keep_ref, bf16[16,128,128]{2,1,0:T(8,128)(2,1)S(1)} %convert_element_type.87.w_ref, ...), custom_call_target="tpu_custom_call" | custom-call | flops 67108864 | bytes 2097152 | tf_op jit(solution)/shard_map/query_sums/pallas_call | solution.py:163
  42.9 2.2 %all-to-all-done.2.q_ref = bf16[32,32,128]{2,1,0:T(8,128)(2,1)S(1)} async-done(((bf16[32,32,128]{2,1,0:T(8,128)(2,1)}), bf16[32,32,128]{2,1,0:T(8,128)(2,1)S(1)}, u32[]{:S(2)}, u32[]{:S(2)}) %all-to-all-start.2) | async-done | bytes 262176 | tf_op jit(solution)/shard_map/all_to_all | solution.py:102
  45.1 7.3 %all-to-all-start.1 = ((bf16[32,32,256]{2,1,0:T(8,128)(2,1)}), bf16[32,32,256]{2,1,0:T(8,128)(2,1)S(1)}, u32[]{:S(2)}, u32[]{:S(2)}) async-start(bf16[32,32,256]{2,1,0:T(8,128)(2,1)} %query_sums.2.after_ref), calls=%async_computation.1 | async-start | bytes 1048576 | tf_op jit(solution)/shard_map/all_to_all | solution.py:102
  52.4 1.2 host_sums.2
  53.6 2.6 %collective-permute-start.1 = (bf16[8,128,256]{2,1,0:T(8,128)(2,1)S(1)}, bf16[8,128,256]{2,1,0:T(8,128)(2,1)S(1)}, u32[]{:S(2)}, u32[]{:S(2)}) collective-permute-start(bf16[8,128,256]{2,1,0:T(8,128)(2,1)S(1)} %get-tuple-element.14), channel_id=1, source_target_pairs={{0,32},{32,0},{64,96},{96,64},{128,160},{160,128},{192,224},{224,1... | collective-permute-start | bytes 1572872 | tf_op jit(solution)/shard_map/ppermute | solution.py:147
  56.2 1.5 collective-permute-done.1
  57.8 2.2 %collective-permute-start.2 = (bf16[4,128,256]{2,1,0:T(8,128)(2,1)S(1)}, bf16[4,128,256]{2,1,0:T(8,128)(2,1)S(1)}, u32[]{:S(2)}, u32[]{:S(2)}) collective-permute-start(bf16[4,128,256]{2,1,0:T(8,128)(2,1)S(1)} %slice.113), channel_id=1, source_target_pairs={{0,64},{32,96},{64,0},{96,32},{128,192},{160,224},{192,128},{224,1... | collective-permute-start | bytes 786440 | tf_op jit(solution)/shard_map/ppermute | solution.py:147
  60.0 8.9 %all-to-all-done.1.in_ref = bf16[32,32,256]{2,1,0:T(8,128)(2,1)S(1)} async-done(((bf16[32,32,256]{2,1,0:T(8,128)(2,1)}), bf16[32,32,256]{2,1,0:T(8,128)(2,1)S(1)}, u32[]{:S(2)}, u32[]{:S(2)}) %all-to-all-start.1) | async-done | bytes 524320 | tf_op jit(solution)/shard_map/all_to_all | solution.py:102
  69.0 0.9 query_update.1
  69.9 5.0 %all-to-all-start.3 = ((bf16[32,32,256]{2,1,0:T(8,128)(2,1)}), bf16[32,32,256]{2,1,0:T(8,128)(2,1)S(1)}, u32[]{:S(2)}, u32[]{:S(2)}) async-start(bf16[32,32,256]{2,1,0:T(8,128)(2,1)} %get-tuple-element.16), calls=%async_computation.3 | async-start | bytes 1048576 | tf_op jit(solution)/shard_map/all_to_all | solution.py:102
  75.0 1.9 %collective-permute-start.3 = (bf16[2,128,256]{2,1,0:T(8,128)(2,1)S(1)}, bf16[2,128,256]{2,1,0:T(8,128)(2,1)S(1)}, u32[]{:S(2)}, u32[]{:S(2)}) collective-permute-start(bf16[2,128,256]{2,1,0:T(8,128)(2,1)S(1)} %slice.114), channel_id=1, source_target_pairs={{0,128},{32,160},{64,192},{96,224},{128,0},{160,32},{192,64},{224,... | collective-permute-start | bytes 393224 | tf_op jit(solution)/shard_map/ppermute | solution.py:147
  77.0 8.3 %collective-permute-done.3 = bf16[2,128,256]{2,1,0:T(8,128)(2,1)S(1)} collective-permute-done((bf16[2,128,256]{2,1,0:T(8,128)(2,1)S(1)}, bf16[2,128,256]{2,1,0:T(8,128)(2,1)S(1)}, u32[]{:S(2)}, u32[]{:S(2)}) %collective-permute-start.3) | collective-permute-done | bytes 131104 | tf_op jit(solution)/shard_map/ppermute | solution.py:147
  85.3 1.9 %collective-permute-start.4 = (bf16[1,128,256]{2,1,0:T(8,128)(2,1)S(1)}, bf16[1,128,256]{2,1,0:T(8,128)(2,1)S(1)}, u32[]{:S(2)}, u32[]{:S(2)}) collective-permute-start(bf16[1,128,256]{2,1,0:T(8,128)(2,1)S(1)} %slice.115), channel_id=1, source_target_pairs={{0,256},{32,288},{64,320},{96,352},{128,384},{160,416},{192,448},{... | collective-permute-start | bytes 196616 | tf_op jit(solution)/shard_map/ppermute | solution.py:147
  87.3 7.5 %collective-permute-done.4 = bf16[1,128,256]{2,1,0:T(8,128)(2,1)S(1)} collective-permute-done((bf16[1,128,256]{2,1,0:T(8,128)(2,1)S(1)}, bf16[1,128,256]{2,1,0:T(8,128)(2,1)S(1)}, u32[]{:S(2)}, u32[]{:S(2)}) %collective-permute-start.4) | collective-permute-done | bytes 65568 | tf_op jit(solution)/shard_map/ppermute | solution.py:147
  94.7 0.9 host_update.1
  95.7 3.5 %all-to-all-start.4 = ((bf16[8,128,256]{2,1,0:T(8,128)(2,1)}), bf16[8,128,256]{2,1,0:T(8,128)(2,1)S(1)}, u32[]{:S(2)}, u32[]{:S(2)}) async-start(bf16[8,128,256]{2,1,0:T(8,128)(2,1)} %get-tuple-element.17.after_ref), calls=%async_computation.4 | async-start | bytes 1048576 | tf_op jit(solution)/shard_map/all_to_all | solution.py:102
  99.2 2.0 %host_sums.3 = (f32[8,128,256]{2,1,0:T(8,128)S(1)}, bf16[8,128,256]{2,1,0:T(8,128)(2,1)}) custom-call(s32[16]{0:T(128)S(1)} %get-tuple-element.38.rows_ref, s32[16]{0:T(128)S(1)} %get-tuple-element.24.slots_ref, f32[2,16]{1,0:T(2,128)S(1)} %multiply_convert_fusion.3.keep_ref, bf16[16,128,128]{2,1,0:T(8,128)(2,1)S(1)} %convert_element_type.87.w_ref, ...), custom_call_target="tpu_custom_call" | custom-call | flops 134217728 | bytes 2097152 | tf_op jit(solution)/shard_map/host_sums/pallas_call | solution.py:153
  101.2 3.8 %collective-permute-start.6 = (bf16[8,128,256]{2,1,0:T(8,128)(2,1)}, bf16[8,128,256]{2,1,0:T(8,128)(2,1)S(1)}, u32[]{:S(2)}, u32[]{:S(2)}) collective-permute-start(bf16[8,128,256]{2,1,0:T(8,128)(2,1)} %get-tuple-element.20), channel_id=1, source_target_pairs={{0,32},{32,0},{64,96},{96,64},{128,160},{160,128},{192,224},{224,1... | collective-permute-start | bytes 1572872 | tf_op jit(solution)/shard_map/ppermute | solution.py:147
  105.0 9.9 %all-to-all-done.4.mine_ref.after_ref = bf16[8,128,256]{2,1,0:T(8,128)(2,1)S(1)} async-done(((bf16[8,128,256]{2,1,0:T(8,128)(2,1)}), bf16[8,128,256]{2,1,0:T(8,128)(2,1)S(1)}, u32[]{:S(2)}, u32[]{:S(2)}) %all-to-all-start.4) | async-done | bytes 524320 | tf_op jit(solution)/shard_map/all_to_all | solution.py:102
  114.9 4.5 %collective-permute-start.5 = (bf16[8,128,256]{2,1,0:T(8,128)(2,1)S(1)}, bf16[8,128,256]{2,1,0:T(8,128)(2,1)S(1)}, u32[]{:S(2)}, u32[]{:S(2)}) collective-permute-start(bf16[8,128,256]{2,1,0:T(8,128)(2,1)S(1)} %all-to-all-done.4.mine_ref.after_ref), channel_id=1, source_target_pairs={{0,32},{32,0},{64,96},{96,64},{128,160},{160,128},{192,224},{224,1... | collective-permute-start | bytes 1572872 | tf_op jit(solution)/shard_map/ppermute | solution.py:147
  119.6 2.2 %collective-permute-start.7 = (bf16[4,128,256]{2,1,0:T(8,128)(2,1)S(1)}, bf16[4,128,256]{2,1,0:T(8,128)(2,1)S(1)}, u32[]{:S(2)}, u32[]{:S(2)}) collective-permute-start(bf16[4,128,256]{2,1,0:T(8,128)(2,1)S(1)} %slice.112), channel_id=1, source_target_pairs={{0,64},{32,96},{64,0},{96,32},{128,192},{160,224},{192,128},{224,1... | collective-permute-start | bytes 786440 | tf_op jit(solution)/shard_map/ppermute | solution.py:147
  121.9 1.9 %query_sums.3.after_ref = bf16[32,32,256]{2,1,0:T(8,128)(2,1)} custom-call(s32[16]{0:T(128)S(1)} %get-tuple-element.38.rows_ref, s32[16]{0:T(128)S(1)} %get-tuple-element.39.slots_ref, f32[2,16]{1,0:T(2,128)S(1)} %multiply_convert_fusion.3.keep_ref, bf16[16,128,128]{2,1,0:T(8,128)(2,1)S(1)} %convert_element_type.87.w_ref, ...), custom_call_target="tpu_custom_call" | custom-call | flops 134217728 | bytes 2097152 | tf_op jit(solution)/shard_map/query_sums/pallas_call | solution.py:163
  123.8 9.3 %all-to-all-start.5 = ((bf16[32,32,256]{2,1,0:T(8,128)(2,1)}), bf16[32,32,256]{2,1,0:T(8,128)(2,1)S(1)}, u32[]{:S(2)}, u32[]{:S(2)}) async-start(bf16[32,32,256]{2,1,0:T(8,128)(2,1)} %query_sums.3.after_ref), calls=%async_computation.5 | async-start | bytes 1048576 | tf_op jit(solution)/shard_map/all_to_all | solution.py:102
  133.2 1.9 %collective-permute-start.10 = (bf16[128,256]{1,0:T(8,128)(2,1)S(1)}, bf16[128,256]{1,0:T(8,128)(2,1)S(1)}, u32[]{:S(2)}, u32[]{:S(2)}) collective-permute-start(bf16[128,256]{1,0:T(8,128)(2,1)S(1)} %get-tuple-element.23), channel_id=1, source_target_pairs={{0,384},{32,416},{64,448},{96,480},{128,256},{160,288},{192,320},{... | collective-permute-start | bytes 196616 | tf_op jit(solution)/shard_map/ppermute | solution.py:218
  135.1 4.8 %collective-permute-start.8 = (bf16[128,256]{1,0:T(8,128)(2,1)S(1)}, bf16[128,256]{1,0:T(8,128)(2,1)S(1)}, u32[]{:S(2)}, u32[]{:S(2)}) collective-permute-start(bf16[128,256]{1,0:T(8,128)(2,1)S(1)} %get-tuple-element.21), channel_id=1, source_target_pairs={{0,256},{32,288},{64,320},{96,352},{128,384},{160,416},{192,448},{... | collective-permute-start | bytes 196616 | tf_op jit(solution)/shard_map/ppermute | solution.py:218
  140.0 4.6 %collective-permute-start.9 = (bf16[128,256]{1,0:T(8,128)(2,1)S(1)}, bf16[128,256]{1,0:T(8,128)(2,1)S(1)}, u32[]{:S(2)}, u32[]{:S(2)}) collective-permute-start(bf16[128,256]{1,0:T(8,128)(2,1)S(1)} %get-tuple-element.22), channel_id=1, source_target_pairs={{0,128},{32,160},{64,192},{96,224},{128,0},{160,32},{192,64},{224,... | collective-permute-start | bytes 196616 | tf_op jit(solution)/shard_map/ppermute | solution.py:218
  144.7 5.5 %collective-permute-done.9 = bf16[128,256]{1,0:T(8,128)(2,1)S(1)} collective-permute-done((bf16[128,256]{1,0:T(8,128)(2,1)S(1)}, bf16[128,256]{1,0:T(8,128)(2,1)S(1)}, u32[]{:S(2)}, u32[]{:S(2)}) %collective-permute-start.9) | collective-permute-done | bytes 65568 | tf_op jit(solution)/shard_map/ppermute | solution.py:218
  (55 shorter events, 7.5 us)
Async XLA Ops:
  1.3 0.8 copy-start
  1.3 0.8 copy-start.1
  1.3 38.6 %copy-start.4 = (s32[16,128,128]{2,1,0:T(8,128)S(1)}, s32[16,128,128]{2,1,0:T(8,128)}, u32[]{:S(2)}) copy-start(s32[16,128,128]{2,1,0:T(8,128)} %param.15) | copy-start | bytes 3145732
  2.9 17.1 %all-to-all-start = ((bf16[8,128,128]{2,1,0:T(8,128)(2,1)}), bf16[8,128,128]{2,1,0:T(8,128)(2,1)S(1)}, u32[]{:S(2)}, u32[]{:S(2)}) async-start(bf16[8,128,128]{2,1,0:T(8,128)(2,1)} %host_spread.1), calls=%async_computation | async-start | bytes 524288 | tf_op jit(solution)/shard_map/all_to_all | solution.py:102
  20.7 24.3 %all-to-all-start.2 = ((bf16[32,32,128]{2,1,0:T(8,128)(2,1)}), bf16[32,32,128]{2,1,0:T(8,128)(2,1)S(1)}, u32[]{:S(2)}, u32[]{:S(2)}) async-start(bf16[32,32,128]{2,1,0:T(8,128)(2,1)} %query_spread.1), calls=%async_computation.2 | async-start | bytes 524288 | tf_op jit(solution)/shard_map/all_to_all | solution.py:102
  34.6 0.7 copy-start.6
  35.2 5.8 %collective-permute-start = (bf16[8,128,128]{2,1,0:T(8,128)(2,1)S(1)}, bf16[8,128,128]{2,1,0:T(8,128)(2,1)S(1)}, u32[]{:S(2)}, u32[]{:S(2)}) collective-permute-start(bf16[8,128,128]{2,1,0:T(8,128)(2,1)S(1)} %all-to-all-done.mine_ref.after_ref), channel_id=1, source_target_pairs={{0,32},{32,0},{64,96},{96,64},{128,160},{160,128},{192,224},{224,1... | collective-permute-start | bytes 786440 | tf_op jit(solution)/shard_map/ppermute | solution.py:147
  39.9 0.7 copy-start.5
  45.1 23.9 %all-to-all-start.1 = ((bf16[32,32,256]{2,1,0:T(8,128)(2,1)}), bf16[32,32,256]{2,1,0:T(8,128)(2,1)S(1)}, u32[]{:S(2)}, u32[]{:S(2)}) async-start(bf16[32,32,256]{2,1,0:T(8,128)(2,1)} %query_sums.2.after_ref), calls=%async_computation.1 | async-start | bytes 1048576 | tf_op jit(solution)/shard_map/all_to_all | solution.py:102
  53.6 4.1 %collective-permute-start.1 = (bf16[8,128,256]{2,1,0:T(8,128)(2,1)S(1)}, bf16[8,128,256]{2,1,0:T(8,128)(2,1)S(1)}, u32[]{:S(2)}, u32[]{:S(2)}) collective-permute-start(bf16[8,128,256]{2,1,0:T(8,128)(2,1)S(1)} %get-tuple-element.14), channel_id=1, source_target_pairs={{0,32},{32,0},{64,96},{96,64},{128,160},{160,128},{192,224},{224,1... | collective-permute-start | bytes 1572872 | tf_op jit(solution)/shard_map/ppermute | solution.py:147
  57.8 17.1 %collective-permute-start.2 = (bf16[4,128,256]{2,1,0:T(8,128)(2,1)S(1)}, bf16[4,128,256]{2,1,0:T(8,128)(2,1)S(1)}, u32[]{:S(2)}, u32[]{:S(2)}) collective-permute-start(bf16[4,128,256]{2,1,0:T(8,128)(2,1)S(1)} %slice.113), channel_id=1, source_target_pairs={{0,64},{32,96},{64,0},{96,32},{128,192},{160,224},{192,128},{224,1... | collective-permute-start | bytes 786440 | tf_op jit(solution)/shard_map/ppermute | solution.py:147
  69.9 24.8 %all-to-all-start.3 = ((bf16[32,32,256]{2,1,0:T(8,128)(2,1)}), bf16[32,32,256]{2,1,0:T(8,128)(2,1)S(1)}, u32[]{:S(2)}, u32[]{:S(2)}) async-start(bf16[32,32,256]{2,1,0:T(8,128)(2,1)} %get-tuple-element.16), calls=%async_computation.3 | async-start | bytes 1048576 | tf_op jit(solution)/shard_map/all_to_all | solution.py:102
  75.0 10.2 %collective-permute-start.3 = (bf16[2,128,256]{2,1,0:T(8,128)(2,1)S(1)}, bf16[2,128,256]{2,1,0:T(8,128)(2,1)S(1)}, u32[]{:S(2)}, u32[]{:S(2)}) collective-permute-start(bf16[2,128,256]{2,1,0:T(8,128)(2,1)S(1)} %slice.114), channel_id=1, source_target_pairs={{0,128},{32,160},{64,192},{96,224},{128,0},{160,32},{192,64},{224,... | collective-permute-start | bytes 393224 | tf_op jit(solution)/shard_map/ppermute | solution.py:147
  85.3 9.4 %collective-permute-start.4 = (bf16[1,128,256]{2,1,0:T(8,128)(2,1)S(1)}, bf16[1,128,256]{2,1,0:T(8,128)(2,1)S(1)}, u32[]{:S(2)}, u32[]{:S(2)}) collective-permute-start(bf16[1,128,256]{2,1,0:T(8,128)(2,1)S(1)} %slice.115), channel_id=1, source_target_pairs={{0,256},{32,288},{64,320},{96,352},{128,384},{160,416},{192,448},{... | collective-permute-start | bytes 196616 | tf_op jit(solution)/shard_map/ppermute | solution.py:147
  95.7 19.3 %all-to-all-start.4 = ((bf16[8,128,256]{2,1,0:T(8,128)(2,1)}), bf16[8,128,256]{2,1,0:T(8,128)(2,1)S(1)}, u32[]{:S(2)}, u32[]{:S(2)}) async-start(bf16[8,128,256]{2,1,0:T(8,128)(2,1)} %get-tuple-element.17.after_ref), calls=%async_computation.4 | async-start | bytes 1048576 | tf_op jit(solution)/shard_map/all_to_all | solution.py:102
  101.2 18.2 %collective-permute-start.6 = (bf16[8,128,256]{2,1,0:T(8,128)(2,1)}, bf16[8,128,256]{2,1,0:T(8,128)(2,1)S(1)}, u32[]{:S(2)}, u32[]{:S(2)}) collective-permute-start(bf16[8,128,256]{2,1,0:T(8,128)(2,1)} %get-tuple-element.20), channel_id=1, source_target_pairs={{0,32},{32,0},{64,96},{96,64},{128,160},{160,128},{192,224},{224,1... | collective-permute-start | bytes 1572872 | tf_op jit(solution)/shard_map/ppermute | solution.py:147
  114.9 7.0 %collective-permute-start.5 = (bf16[8,128,256]{2,1,0:T(8,128)(2,1)S(1)}, bf16[8,128,256]{2,1,0:T(8,128)(2,1)S(1)}, u32[]{:S(2)}, u32[]{:S(2)}) collective-permute-start(bf16[8,128,256]{2,1,0:T(8,128)(2,1)S(1)} %all-to-all-done.4.mine_ref.after_ref), channel_id=1, source_target_pairs={{0,32},{32,0},{64,96},{96,64},{128,160},{160,128},{192,224},{224,1... | collective-permute-start | bytes 1572872 | tf_op jit(solution)/shard_map/ppermute | solution.py:147
  119.6 2.3 %copy-start.2 = (f32[8,128,256]{2,1,0:T(8,128)}, f32[8,128,256]{2,1,0:T(8,128)S(1)}, u32[]{:S(2)}) copy-start(f32[8,128,256]{2,1,0:T(8,128)S(1)} %convert_add_fusion) | copy-start | bytes 3145732
  119.6 13.5 %collective-permute-start.7 = (bf16[4,128,256]{2,1,0:T(8,128)(2,1)S(1)}, bf16[4,128,256]{2,1,0:T(8,128)(2,1)S(1)}, u32[]{:S(2)}, u32[]{:S(2)}) collective-permute-start(bf16[4,128,256]{2,1,0:T(8,128)(2,1)S(1)} %slice.112), channel_id=1, source_target_pairs={{0,64},{32,96},{64,0},{96,32},{128,192},{160,224},{192,128},{224,1... | collective-permute-start | bytes 786440 | tf_op jit(solution)/shard_map/ppermute | solution.py:147
  123.8 9.3 %copy-start.3 = (f32[8,128,256]{2,1,0:T(8,128)S(1)}, f32[8,128,256]{2,1,0:T(8,128)}, u32[]{:S(2)}) copy-start(f32[8,128,256]{2,1,0:T(8,128)} %copy-done.2) | copy-start | bytes 3145732
  123.8 27.1 %all-to-all-start.5 = ((bf16[32,32,256]{2,1,0:T(8,128)(2,1)}), bf16[32,32,256]{2,1,0:T(8,128)(2,1)S(1)}, u32[]{:S(2)}, u32[]{:S(2)}) async-start(bf16[32,32,256]{2,1,0:T(8,128)(2,1)} %query_sums.3.after_ref), calls=%async_computation.5 | async-start | bytes 1048576 | tf_op jit(solution)/shard_map/all_to_all | solution.py:102
  133.2 11.4 %collective-permute-start.10 = (bf16[128,256]{1,0:T(8,128)(2,1)S(1)}, bf16[128,256]{1,0:T(8,128)(2,1)S(1)}, u32[]{:S(2)}, u32[]{:S(2)}) collective-permute-start(bf16[128,256]{1,0:T(8,128)(2,1)S(1)} %get-tuple-element.23), channel_id=1, source_target_pairs={{0,384},{32,416},{64,448},{96,480},{128,256},{160,288},{192,320},{... | collective-permute-start | bytes 196616 | tf_op jit(solution)/shard_map/ppermute | solution.py:218
  135.1 9.5 %collective-permute-start.8 = (bf16[128,256]{1,0:T(8,128)(2,1)S(1)}, bf16[128,256]{1,0:T(8,128)(2,1)S(1)}, u32[]{:S(2)}, u32[]{:S(2)}) collective-permute-start(bf16[128,256]{1,0:T(8,128)(2,1)S(1)} %get-tuple-element.21), channel_id=1, source_target_pairs={{0,256},{32,288},{64,320},{96,352},{128,384},{160,416},{192,448},{... | collective-permute-start | bytes 196616 | tf_op jit(solution)/shard_map/ppermute | solution.py:218
  140.0 10.2 %collective-permute-start.9 = (bf16[128,256]{1,0:T(8,128)(2,1)S(1)}, bf16[128,256]{1,0:T(8,128)(2,1)S(1)}, u32[]{:S(2)}, u32[]{:S(2)}) collective-permute-start(bf16[128,256]{1,0:T(8,128)(2,1)S(1)} %get-tuple-element.22), channel_id=1, source_target_pairs={{0,128},{32,160},{64,192},{96,224},{128,0},{160,32},{192,64},{224,... | collective-permute-start | bytes 196616 | tf_op jit(solution)/shard_map/ppermute | solution.py:218

commit v4 on v3

--- a/solution.py
+++ b/solution.py
@@ -102,8 +102,8 @@
     return lax.all_to_all(blocks, axis, 0, 0, axis_index_groups=groups, tiled=True)
 
 
-def reverse_bits(index, bits):
-    return sum(((index >> b) & 1) << (bits - 1 - b) for b in range(bits))
+def place(index, order):
+    return sum(((index >> b) & 1) << (len(order) - 1 - i) for i, b in enumerate(order))
 
 
 def split_views(both):
@@ -131,8 +131,8 @@
     rows = tile_rows % slab_blocks
     cols = tile_cols // n_ha
     slots = ((cols % 2) ^ core) * chips + cols // 2
-    bits = n_pb.bit_length() - 1
-    by_bits = reverse_bits(cols ^ lax.axis_index("pb"), bits)
+    halving_0, halving_1 = (0, 3, 1, 2), (0, 2, 1, 3)
+    away = cols ^ lax.axis_index("pb")
     live = jnp.arange(CAP, dtype=jnp.int32) < live_tiles[0]
     keep = (keep_mask * live[None]).astype(jnp.float32)
     weights = tile_counts.astype(jnp.bfloat16)
@@ -149,7 +149,7 @@
     def swap_core(blocks):
         return swap(blocks, "pb", 0)
 
-    def host_sums(slab, after):
+    def host_sums(slab, halving, after):
         return call(
             host_kernel,
             "host_sums",
@@ -157,7 +157,7 @@
             [SMEM, SMEM, SMEM, VMEM, VMEM, ANY],
             [pltpu.VMEM((n_pb, BLOCK, BOTH), jnp.float32)],
             2 * CAP * BLOCK * BLOCK * slab.shape[2],
-        )(rows, by_bits, keep, weights, slab, after)
+        )(rows, place(away, halving), keep, weights, slab, after)
 
     def query_sums(mine, slots, after):
         return call(
@@ -169,20 +169,9 @@
             2 * CAP * BLOCK * BLOCK * mine.shape[2],
         )(rows, slots, keep, weights, mine, swap_core(mine), after)
 
-    def gather_steps(block):
-        steps = [block[None]]
-        for bit in range(bits - 1, 0, -1):
-            steps.append(jnp.concatenate([steps[-1], swap(steps[-1], "pb", bit)]))
-        return steps
-
-    def reduce_steps(own, send):
-        steps = [own + swap_core(send).astype(jnp.float32)]
-        for bit in range(1, bits):
-            total = steps[-1]
-            size = total.shape[0] // 2
-            other = swap(total[size:].astype(jnp.bfloat16), "pb", bit)
-            steps.append(total[:size] + other.astype(jnp.float32))
-        return steps
+    def halve(total, bit):
+        size = total.shape[0] // 2
+        return total[:size] + swap(total[size:].astype(jnp.bfloat16), "pb", bit).astype(jnp.float32)
 
     def update(name, arrived, scale, copies, after):
         shape = arrived.shape[1:]
@@ -199,23 +188,26 @@
     slab = exchange(spread("query_spread", scale_query, query_embed, n_ha, mine), "ha")
     part = query_sums(mine, slots, mine)
     arrived = exchange(part, "ha")
-    sums_0 = reduce_steps(*host_sums(slab, part))
-    query_1, copies = update("query_update", arrived, scale_query, n_ha, sums_0[0])
+    own, send = host_sums(slab, halving_0, part)
+    cores = own + swap_core(send).astype(jnp.float32)
+    total = cores
+    for bit in halving_0[1:]:
+        total = halve(total, bit)
+    query_1, copies = update("query_update", arrived, scale_query, n_ha, cores)
 
     slab = exchange(copies, "ha")
-    host_1, copies = update("host_update", sums_0[-1], scale_host, chips, slab)
+    host_1, copies = update("host_update", total, scale_host, chips, slab)
     mine = exchange(copies, "pb", same_core)
-    own, send = host_sums(slab, copies)
-    total = own + swap_core(send).astype(jnp.float32)
-    size = total.shape[0] // 2
-    total = total[:size] + swap(total[size:].astype(jnp.bfloat16), "pb", 1).astype(jnp.float32)
+    own, send = host_sums(slab, halving_1, copies)
+    total = halve(own + swap_core(send).astype(jnp.float32), halving_1[1])
     part = query_sums(mine, slots, mine)
     arrived = exchange(part, "ha")
-    blocks = call(cast_kernel, "cast", (half(BLOCK, BOTH),) * (size - 1), [VMEM, ANY])(total, part)
+    blocks = (half(BLOCK, BOTH),) * (total.shape[0] - 1)
+    blocks = call(cast_kernel, "cast", blocks, [VMEM, ANY])(total, part)
     host_sum = total[0]
     for index, block in enumerate(blocks, 1):
-        away = reverse_bits(index, bits - 2) << 2
-        other = lax.ppermute(block, "pb", [(i, i ^ away) for i in range(n_pb)])
+        across = ((index >> 1) << halving_1[2]) | ((index & 1) << halving_1[3])
+        other = lax.ppermute(block, "pb", [(i, i ^ across) for i in range(n_pb)])
         host_sum = host_sum + other.astype(jnp.float32)
     host_2 = sent(scale_host, host_sum)
     query_2 = sent(scale_query, jnp.sum(arrived.astype(jnp.float32), axis=0))

time: 153 us -> 148 us (0.967)
  waiting for transfers between devices: 51.6 us -> 39.3 us
  starting transfers between devices: 81.8 us -> 89.9 us
    ppermute x8, starting transfers between devices: 23.8 us -> 31.7 us  [swap(): return lax.ppermute(blocks, axis, [(i, i ^ 1 << bit) for i in range(size)])]
    ppermute x8, waiting for transfers between devices: 17.7 us -> 12.1 us  [swap(): return lax.ppermute(blocks, axis, [(i, i ^ 1 << bit) for i in range(size)])]
    ppermute x3, waiting for transfers between devices: 5.5 us -> 2.08 us  [per_device(): other = lax.ppermute(block, 'pb', [(i, i ^ across) for i in range(n_pb)])]
    all_to_all x6, waiting for transfers between devices: 28.3 us -> 25.1 us  [exchange(): lax.all_to_all(blocks, axis, 0, 0, axis_index_groups=groups, tiled=True)]
  transfers between devices with their start and end apart: 17 -> 17, of which waited for: 9 -> 11; matrix products, arithmetic and copies ran while one was open for 2% -> 1% of each run, Pallas kernels for 5% -> 5%
where the time goes in v4:
time: 148 us; the launch traced here: 146 us
  starting transfers between devices  89.9 us (61%)
  waiting for transfers between devices  39.3 us (27%)
  Pallas kernels  10.4 us (7%)
  other arithmetic  3.41 us (2%)
  between operations  1.68 us (1%)
  local copies, waits for them, and re-layouts  1.63 us (1%)
    all_to_all x6, starting transfers between devices, exchange(): lax.all_to_all(blocks, axis, 0, 0, axis_index_groups=groups, tiled=True)  46.8 us
    ppermute x8, starting transfers between devices, swap(): return lax.ppermute(blocks, axis, [(i, i ^ 1 << bit) for i in range(size)])  31.7 us
    all_to_all x6, waiting for transfers between devices, exchange(): lax.all_to_all(blocks, axis, 0, 0, axis_index_groups=groups, tiled=True)  25.1 us
    ppermute x8, waiting for transfers between devices, swap(): return lax.ppermute(blocks, axis, [(i, i ^ 1 << bit) for i in range(size)])  12.1 us
    ppermute x3, starting transfers between devices, per_device(): other = lax.ppermute(block, 'pb', [(i, i ^ across) for i in range(n_pb)])  11.4 us
    pallas_call x2, Pallas kernels, query_sums(): call(query_kernel, 'query_sums', half(n_ha, local, BOTH), [SMEM, SMEM, SM...  3.74 us
    pallas_call x2, Pallas kernels, host_sums(): call(host_kernel, 'host_sums', (single(chips, BLOCK, BOTH), half(chips, B...  3.23 us
  transfers between devices with their start and end apart: 17, of which 11 were waited for; matrix products, arithmetic and copies ran while one was open for 1% of the time, Pallas kernels for 5%

profile of v4, /device:TPU:1, one launch (start us, length us, event | category | flops | bytes accessed | tf_op | source)
XLA Modules:
  0.0 146.3 jit_solution(3074816920658753302)
XLA Ops:
  2.8 7.7 %all-to-all-start = ((bf16[8,128,128]{2,1,0:T(8,128)(2,1)}), bf16[8,128,128]{2,1,0:T(8,128)(2,1)S(1)}, u32[]{:S(2)}, u32[]{:S(2)}) async-start(bf16[8,128,128]{2,1,0:T(8,128)(2,1)} %host_spread.1), calls=%async_computation | async-start | bytes 524288 | tf_op jit(solution)/shard_map/all_to_all | solution.py:102
  11.9 8.0 %all-to-all-done.mine_ref.after_ref = bf16[8,128,128]{2,1,0:T(8,128)(2,1)S(1)} async-done(((bf16[8,128,128]{2,1,0:T(8,128)(2,1)}), bf16[8,128,128]{2,1,0:T(8,128)(2,1)S(1)}, u32[]{:S(2)}, u32[]{:S(2)}) %all-to-all-start) | async-done | bytes 262176 | tf_op jit(solution)/shard_map/all_to_all | solution.py:102
  20.7 14.0 %all-to-all-start.2 = ((bf16[32,32,128]{2,1,0:T(8,128)(2,1)}), bf16[32,32,128]{2,1,0:T(8,128)(2,1)S(1)}, u32[]{:S(2)}, u32[]{:S(2)}) async-start(bf16[32,32,128]{2,1,0:T(8,128)(2,1)} %query_spread.1), calls=%async_computation.2 | async-start | bytes 524288 | tf_op jit(solution)/shard_map/all_to_all | solution.py:102
  34.7 4.7 %collective-permute-start = (bf16[8,128,128]{2,1,0:T(8,128)(2,1)S(1)}, bf16[8,128,128]{2,1,0:T(8,128)(2,1)S(1)}, u32[]{:S(2)}, u32[]{:S(2)}) collective-permute-start(bf16[8,128,128]{2,1,0:T(8,128)(2,1)S(1)} %all-to-all-done.mine_ref.after_ref), channel_id=1, source_target_pairs={{0,32},{32,0},{64,96},{96,64},{128,160},{160,128},{192,224},{224,1... | collective-permute-start | bytes 786440 | tf_op jit(solution)/shard_map/ppermute | solution.py:147
  40.5 1.8 %query_sums.2.after_ref = bf16[32,32,256]{2,1,0:T(8,128)(2,1)} custom-call(s32[16]{0:T(128)S(1)} %get-tuple-element.40.rows_ref, s32[16]{0:T(128)S(1)} %get-tuple-element.39.slots_ref, f32[2,16]{1,0:T(2,128)S(1)} %multiply_convert_fusion.3.keep_ref, bf16[16,128,128]{2,1,0:T(8,128)(2,1)S(1)} %convert_element_type.87.w_ref, ...), custom_call_target="tpu_custom_call" | custom-call | flops 67108864 | bytes 2097152 | tf_op jit(solution)/shard_map/query_sums/pallas_call | solution.py:163
  42.4 2.8 %all-to-all-done.2.q_ref = bf16[32,32,128]{2,1,0:T(8,128)(2,1)S(1)} async-done(((bf16[32,32,128]{2,1,0:T(8,128)(2,1)}), bf16[32,32,128]{2,1,0:T(8,128)(2,1)S(1)}, u32[]{:S(2)}, u32[]{:S(2)}) %all-to-all-start.2) | async-done | bytes 262176 | tf_op jit(solution)/shard_map/all_to_all | solution.py:102
  45.2 6.7 %all-to-all-start.1 = ((bf16[32,32,256]{2,1,0:T(8,128)(2,1)}), bf16[32,32,256]{2,1,0:T(8,128)(2,1)S(1)}, u32[]{:S(2)}, u32[]{:S(2)}) async-start(bf16[32,32,256]{2,1,0:T(8,128)(2,1)} %query_sums.2.after_ref), calls=%async_computation.1 | async-start | bytes 1048576 | tf_op jit(solution)/shard_map/all_to_all | solution.py:102
  51.9 1.2 host_sums.2
  53.1 3.0 %collective-permute-start.1 = (bf16[8,128,256]{2,1,0:T(8,128)(2,1)S(1)}, bf16[8,128,256]{2,1,0:T(8,128)(2,1)S(1)}, u32[]{:S(2)}, u32[]{:S(2)}) collective-permute-start(bf16[8,128,256]{2,1,0:T(8,128)(2,1)S(1)} %get-tuple-element.14), channel_id=1, source_target_pairs={{0,32},{32,0},{64,96},{96,64},{128,160},{160,128},{192,224},{224,1... | collective-permute-start | bytes 1572872 | tf_op jit(solution)/shard_map/ppermute | solution.py:147
  56.1 1.5 %collective-permute-done.1 = bf16[8,128,256]{2,1,0:T(8,128)(2,1)S(1)} collective-permute-done((bf16[8,128,256]{2,1,0:T(8,128)(2,1)S(1)}, bf16[8,128,256]{2,1,0:T(8,128)(2,1)S(1)}, u32[]{:S(2)}, u32[]{:S(2)}) %collective-permute-start.1) | collective-permute-done | bytes 524320 | tf_op jit(solution)/shard_map/ppermute | solution.py:147
  57.8 2.9 %collective-permute-start.2 = (bf16[4,128,256]{2,1,0:T(8,128)(2,1)S(1)}, bf16[4,128,256]{2,1,0:T(8,128)(2,1)S(1)}, u32[]{:S(2)}, u32[]{:S(2)}) collective-permute-start(bf16[4,128,256]{2,1,0:T(8,128)(2,1)S(1)} %slice.113), channel_id=1, source_target_pairs={{0,256},{32,288},{64,320},{96,352},{128,384},{160,416},{192,448},{... | collective-permute-start | bytes 786440 | tf_op jit(solution)/shard_map/ppermute | solution.py:147
  60.7 6.7 %all-to-all-done.1.in_ref = bf16[32,32,256]{2,1,0:T(8,128)(2,1)S(1)} async-done(((bf16[32,32,256]{2,1,0:T(8,128)(2,1)}), bf16[32,32,256]{2,1,0:T(8,128)(2,1)S(1)}, u32[]{:S(2)}, u32[]{:S(2)}) %all-to-all-start.1) | async-done | bytes 524320 | tf_op jit(solution)/shard_map/all_to_all | solution.py:102
  67.4 0.9 query_update.1
  68.3 5.9 %all-to-all-start.3 = ((bf16[32,32,256]{2,1,0:T(8,128)(2,1)}), bf16[32,32,256]{2,1,0:T(8,128)(2,1)S(1)}, u32[]{:S(2)}, u32[]{:S(2)}) async-start(bf16[32,32,256]{2,1,0:T(8,128)(2,1)} %get-tuple-element.16), calls=%async_computation.3 | async-start | bytes 1048576 | tf_op jit(solution)/shard_map/all_to_all | solution.py:102
  74.4 5.5 %collective-permute-start.3 = (bf16[2,128,256]{2,1,0:T(8,128)(2,1)S(1)}, bf16[2,128,256]{2,1,0:T(8,128)(2,1)S(1)}, u32[]{:S(2)}, u32[]{:S(2)}) collective-permute-start(bf16[2,128,256]{2,1,0:T(8,128)(2,1)S(1)} %slice.114), channel_id=1, source_target_pairs={{0,64},{32,96},{64,0},{96,32},{128,192},{160,224},{192,128},{224,1... | collective-permute-start | bytes 393224 | tf_op jit(solution)/shard_map/ppermute | solution.py:147
  79.8 2.3 %collective-permute-done.3 = bf16[2,128,256]{2,1,0:T(8,128)(2,1)S(1)} collective-permute-done((bf16[2,128,256]{2,1,0:T(8,128)(2,1)S(1)}, bf16[2,128,256]{2,1,0:T(8,128)(2,1)S(1)}, u32[]{:S(2)}, u32[]{:S(2)}) %collective-permute-start.3) | collective-permute-done | bytes 131104 | tf_op jit(solution)/shard_map/ppermute | solution.py:147
  82.2 2.2 %collective-permute-start.4 = (bf16[1,128,256]{2,1,0:T(8,128)(2,1)S(1)}, bf16[1,128,256]{2,1,0:T(8,128)(2,1)S(1)}, u32[]{:S(2)}, u32[]{:S(2)}) collective-permute-start(bf16[1,128,256]{2,1,0:T(8,128)(2,1)S(1)} %slice.115), channel_id=1, source_target_pairs={{0,128},{32,160},{64,192},{96,224},{128,0},{160,32},{192,64},{224,... | collective-permute-start | bytes 196616 | tf_op jit(solution)/shard_map/ppermute | solution.py:147
  84.5 4.0 %collective-permute-done.4 = bf16[1,128,256]{2,1,0:T(8,128)(2,1)S(1)} collective-permute-done((bf16[1,128,256]{2,1,0:T(8,128)(2,1)S(1)}, bf16[1,128,256]{2,1,0:T(8,128)(2,1)S(1)}, u32[]{:S(2)}, u32[]{:S(2)}) %collective-permute-start.4) | collective-permute-done | bytes 65568 | tf_op jit(solution)/shard_map/ppermute | solution.py:147
  89.3 0.9 host_update.1
  90.2 3.8 %all-to-all-start.4 = ((bf16[8,128,256]{2,1,0:T(8,128)(2,1)}), bf16[8,128,256]{2,1,0:T(8,128)(2,1)S(1)}, u32[]{:S(2)}, u32[]{:S(2)}) async-start(bf16[8,128,256]{2,1,0:T(8,128)(2,1)} %get-tuple-element.17.after_ref), calls=%async_computation.4 | async-start | bytes 1048576 | tf_op jit(solution)/shard_map/all_to_all | solution.py:102
  94.0 2.0 %host_sums.3 = (f32[8,128,256]{2,1,0:T(8,128)S(1)}, bf16[8,128,256]{2,1,0:T(8,128)(2,1)}) custom-call(s32[16]{0:T(128)S(1)} %get-tuple-element.40.rows_ref, s32[16]{0:T(128)S(1)} %get-tuple-element.24.slots_ref, f32[2,16]{1,0:T(2,128)S(1)} %multiply_convert_fusion.3.keep_ref, bf16[16,128,128]{2,1,0:T(8,128)(2,1)S(1)} %convert_element_type.87.w_ref, ...), custom_call_target="tpu_custom_call" | custom-call | flops 134217728 | bytes 2097152 | tf_op jit(solution)/shard_map/host_sums/pallas_call | solution.py:153
  96.0 5.4 %collective-permute-start.6 = (bf16[8,128,256]{2,1,0:T(8,128)(2,1)}, bf16[8,128,256]{2,1,0:T(8,128)(2,1)S(1)}, u32[]{:S(2)}, u32[]{:S(2)}) collective-permute-start(bf16[8,128,256]{2,1,0:T(8,128)(2,1)} %get-tuple-element.20), channel_id=1, source_target_pairs={{0,32},{32,0},{64,96},{96,64},{128,160},{160,128},{192,224},{224,1... | collective-permute-start | bytes 1572872 | tf_op jit(solution)/shard_map/ppermute | solution.py:147
  101.4 6.7 %all-to-all-done.4.mine_ref.after_ref = bf16[8,128,256]{2,1,0:T(8,128)(2,1)S(1)} async-done(((bf16[8,128,256]{2,1,0:T(8,128)(2,1)}), bf16[8,128,256]{2,1,0:T(8,128)(2,1)S(1)}, u32[]{:S(2)}, u32[]{:S(2)}) %all-to-all-start.4) | async-done | bytes 524320 | tf_op jit(solution)/shard_map/all_to_all | solution.py:102
  108.1 6.2 %collective-permute-start.5 = (bf16[8,128,256]{2,1,0:T(8,128)(2,1)S(1)}, bf16[8,128,256]{2,1,0:T(8,128)(2,1)S(1)}, u32[]{:S(2)}, u32[]{:S(2)}) collective-permute-start(bf16[8,128,256]{2,1,0:T(8,128)(2,1)S(1)} %all-to-all-done.4.mine_ref.after_ref), channel_id=1, source_target_pairs={{0,32},{32,0},{64,96},{96,64},{128,160},{160,128},{192,224},{224,1... | collective-permute-start | bytes 1572872 | tf_op jit(solution)/shard_map/ppermute | solution.py:147
  114.5 1.9 %collective-permute-start.7 = (bf16[4,128,256]{2,1,0:T(8,128)(2,1)S(1)}, bf16[4,128,256]{2,1,0:T(8,128)(2,1)S(1)}, u32[]{:S(2)}, u32[]{:S(2)}) collective-permute-start(bf16[4,128,256]{2,1,0:T(8,128)(2,1)S(1)} %slice.112), channel_id=1, source_target_pairs={{0,128},{32,160},{64,192},{96,224},{128,0},{160,32},{192,64},{224,... | collective-permute-start | bytes 786440 | tf_op jit(solution)/shard_map/ppermute | solution.py:147
  116.5 1.9 %query_sums.3.after_ref = bf16[32,32,256]{2,1,0:T(8,128)(2,1)} custom-call(s32[16]{0:T(128)S(1)} %get-tuple-element.40.rows_ref, s32[16]{0:T(128)S(1)} %get-tuple-element.39.slots_ref, f32[2,16]{1,0:T(2,128)S(1)} %multiply_convert_fusion.3.keep_ref, bf16[16,128,128]{2,1,0:T(8,128)(2,1)S(1)} %convert_element_type.87.w_ref, ...), custom_call_target="tpu_custom_call" | custom-call | flops 134217728 | bytes 2097152 | tf_op jit(solution)/shard_map/query_sums/pallas_call | solution.py:163
  118.4 8.8 %all-to-all-start.5 = ((bf16[32,32,256]{2,1,0:T(8,128)(2,1)}), bf16[32,32,256]{2,1,0:T(8,128)(2,1)S(1)}, u32[]{:S(2)}, u32[]{:S(2)}) async-start(bf16[32,32,256]{2,1,0:T(8,128)(2,1)} %query_sums.3.after_ref), calls=%async_computation.5 | async-start | bytes 1048576 | tf_op jit(solution)/shard_map/all_to_all | solution.py:102
  127.2 4.0 %collective-permute-done.7 = bf16[4,128,256]{2,1,0:T(8,128)(2,1)S(1)} collective-permute-done((bf16[4,128,256]{2,1,0:T(8,128)(2,1)S(1)}, bf16[4,128,256]{2,1,0:T(8,128)(2,1)S(1)}, u32[]{:S(2)}, u32[]{:S(2)}) %collective-permute-start.7) | collective-permute-done | bytes 262176 | tf_op jit(solution)/shard_map/ppermute | solution.py:147
  131.2 1.9 %collective-permute-start.10 = (bf16[128,256]{1,0:T(8,128)(2,1)S(1)}, bf16[128,256]{1,0:T(8,128)(2,1)S(1)}, u32[]{:S(2)}, u32[]{:S(2)}) collective-permute-start(bf16[128,256]{1,0:T(8,128)(2,1)S(1)} %get-tuple-element.23), channel_id=1, source_target_pairs={{0,320},{32,352},{64,256},{96,288},{128,448},{160,480},{192,384},{... | collective-permute-start | bytes 196616 | tf_op jit(solution)/shard_map/ppermute | solution.py:210
  133.2 3.2 %collective-permute-start.8 = (bf16[128,256]{1,0:T(8,128)(2,1)S(1)}, bf16[128,256]{1,0:T(8,128)(2,1)S(1)}, u32[]{:S(2)}, u32[]{:S(2)}) collective-permute-start(bf16[128,256]{1,0:T(8,128)(2,1)S(1)} %get-tuple-element.21), channel_id=1, source_target_pairs={{0,256},{32,288},{64,320},{96,352},{128,384},{160,416},{192,448},{... | collective-permute-start | bytes 196616 | tf_op jit(solution)/shard_map/ppermute | solution.py:210
  136.4 6.3 %collective-permute-start.9 = (bf16[128,256]{1,0:T(8,128)(2,1)S(1)}, bf16[128,256]{1,0:T(8,128)(2,1)S(1)}, u32[]{:S(2)}, u32[]{:S(2)}) collective-permute-start(bf16[128,256]{1,0:T(8,128)(2,1)S(1)} %get-tuple-element.22), channel_id=1, source_target_pairs={{0,64},{32,96},{64,0},{96,32},{128,192},{160,224},{192,128},{224,1... | collective-permute-start | bytes 196616 | tf_op jit(solution)/shard_map/ppermute | solution.py:210
  142.7 2.1 %collective-permute-done.9 = bf16[128,256]{1,0:T(8,128)(2,1)S(1)} collective-permute-done((bf16[128,256]{1,0:T(8,128)(2,1)S(1)}, bf16[128,256]{1,0:T(8,128)(2,1)S(1)}, u32[]{:S(2)}, u32[]{:S(2)}) %collective-permute-start.9) | collective-permute-done | bytes 65568 | tf_op jit(solution)/shard_map/ppermute | solution.py:210
  (57 shorter events, 7.8 us)
Async XLA Ops:
  1.3 0.8 copy-start
  1.3 0.8 copy-start.1
  1.3 38.1 %copy-start.4 = (s32[16,128,128]{2,1,0:T(8,128)S(1)}, s32[16,128,128]{2,1,0:T(8,128)}, u32[]{:S(2)}) copy-start(s32[16,128,128]{2,1,0:T(8,128)} %param.15) | copy-start | bytes 3145732
  2.8 17.1 %all-to-all-start = ((bf16[8,128,128]{2,1,0:T(8,128)(2,1)}), bf16[8,128,128]{2,1,0:T(8,128)(2,1)S(1)}, u32[]{:S(2)}, u32[]{:S(2)}) async-start(bf16[8,128,128]{2,1,0:T(8,128)(2,1)} %host_spread.1), calls=%async_computation | async-start | bytes 524288 | tf_op jit(solution)/shard_map/all_to_all | solution.py:102
  20.7 14.0 %copy-start.5 = (s32[2,16]{1,0:T(2,128)S(1)}, s32[2,16]{1,0:T(2,128)}, u32[]{:S(2)}) copy-start(s32[2,16]{1,0:T(2,128)} %param.16) | copy-start | bytes 388
  20.7 24.5 %all-to-all-start.2 = ((bf16[32,32,128]{2,1,0:T(8,128)(2,1)}), bf16[32,32,128]{2,1,0:T(8,128)(2,1)S(1)}, u32[]{:S(2)}, u32[]{:S(2)}) async-start(bf16[32,32,128]{2,1,0:T(8,128)(2,1)} %query_spread.1), calls=%async_computation.2 | async-start | bytes 524288 | tf_op jit(solution)/shard_map/all_to_all | solution.py:102
  34.7 4.7 %copy-start.7 = (s32[16]{0:T(128)S(1)}, s32[16]{0:T(128)}, u32[]{:S(2)}) copy-start(s32[16]{0:T(128)} %param.14) | copy-start | bytes 196
  34.7 5.8 %collective-permute-start = (bf16[8,128,128]{2,1,0:T(8,128)(2,1)S(1)}, bf16[8,128,128]{2,1,0:T(8,128)(2,1)S(1)}, u32[]{:S(2)}, u32[]{:S(2)}) collective-permute-start(bf16[8,128,128]{2,1,0:T(8,128)(2,1)S(1)} %all-to-all-done.mine_ref.after_ref), channel_id=1, source_target_pairs={{0,32},{32,0},{64,96},{96,64},{128,160},{160,128},{192,224},{224,1... | collective-permute-start | bytes 786440 | tf_op jit(solution)/shard_map/ppermute | solution.py:147
  39.6 0.7 copy-start.6
  45.2 22.2 %all-to-all-start.1 = ((bf16[32,32,256]{2,1,0:T(8,128)(2,1)}), bf16[32,32,256]{2,1,0:T(8,128)(2,1)S(1)}, u32[]{:S(2)}, u32[]{:S(2)}) async-start(bf16[32,32,256]{2,1,0:T(8,128)(2,1)} %query_sums.2.after_ref), calls=%async_computation.1 | async-start | bytes 1048576 | tf_op jit(solution)/shard_map/all_to_all | solution.py:102
  53.1 4.5 %collective-permute-start.1 = (bf16[8,128,256]{2,1,0:T(8,128)(2,1)S(1)}, bf16[8,128,256]{2,1,0:T(8,128)(2,1)S(1)}, u32[]{:S(2)}, u32[]{:S(2)}) collective-permute-start(bf16[8,128,256]{2,1,0:T(8,128)(2,1)S(1)} %get-tuple-element.14), channel_id=1, source_target_pairs={{0,32},{32,0},{64,96},{96,64},{128,160},{160,128},{192,224},{224,1... | collective-permute-start | bytes 1572872 | tf_op jit(solution)/shard_map/ppermute | solution.py:147
  57.8 16.5 %collective-permute-start.2 = (bf16[4,128,256]{2,1,0:T(8,128)(2,1)S(1)}, bf16[4,128,256]{2,1,0:T(8,128)(2,1)S(1)}, u32[]{:S(2)}, u32[]{:S(2)}) collective-permute-start(bf16[4,128,256]{2,1,0:T(8,128)(2,1)S(1)} %slice.113), channel_id=1, source_target_pairs={{0,256},{32,288},{64,320},{96,352},{128,384},{160,416},{192,448},{... | collective-permute-start | bytes 786440 | tf_op jit(solution)/shard_map/ppermute | solution.py:147
  68.3 21.0 %all-to-all-start.3 = ((bf16[32,32,256]{2,1,0:T(8,128)(2,1)}), bf16[32,32,256]{2,1,0:T(8,128)(2,1)S(1)}, u32[]{:S(2)}, u32[]{:S(2)}) async-start(bf16[32,32,256]{2,1,0:T(8,128)(2,1)} %get-tuple-element.16), calls=%async_computation.3 | async-start | bytes 1048576 | tf_op jit(solution)/shard_map/all_to_all | solution.py:102
  74.4 7.8 %collective-permute-start.3 = (bf16[2,128,256]{2,1,0:T(8,128)(2,1)S(1)}, bf16[2,128,256]{2,1,0:T(8,128)(2,1)S(1)}, u32[]{:S(2)}, u32[]{:S(2)}) collective-permute-start(bf16[2,128,256]{2,1,0:T(8,128)(2,1)S(1)} %slice.114), channel_id=1, source_target_pairs={{0,64},{32,96},{64,0},{96,32},{128,192},{160,224},{192,128},{224,1... | collective-permute-start | bytes 393224 | tf_op jit(solution)/shard_map/ppermute | solution.py:147
  82.2 6.2 %collective-permute-start.4 = (bf16[1,128,256]{2,1,0:T(8,128)(2,1)S(1)}, bf16[1,128,256]{2,1,0:T(8,128)(2,1)S(1)}, u32[]{:S(2)}, u32[]{:S(2)}) collective-permute-start(bf16[1,128,256]{2,1,0:T(8,128)(2,1)S(1)} %slice.115), channel_id=1, source_target_pairs={{0,128},{32,160},{64,192},{96,224},{128,0},{160,32},{192,64},{224,... | collective-permute-start | bytes 196616 | tf_op jit(solution)/shard_map/ppermute | solution.py:147
  90.2 17.9 %all-to-all-start.4 = ((bf16[8,128,256]{2,1,0:T(8,128)(2,1)}), bf16[8,128,256]{2,1,0:T(8,128)(2,1)S(1)}, u32[]{:S(2)}, u32[]{:S(2)}) async-start(bf16[8,128,256]{2,1,0:T(8,128)(2,1)} %get-tuple-element.17.after_ref), calls=%async_computation.4 | async-start | bytes 1048576 | tf_op jit(solution)/shard_map/all_to_all | solution.py:102
  96.0 18.3 %collective-permute-start.6 = (bf16[8,128,256]{2,1,0:T(8,128)(2,1)}, bf16[8,128,256]{2,1,0:T(8,128)(2,1)S(1)}, u32[]{:S(2)}, u32[]{:S(2)}) collective-permute-start(bf16[8,128,256]{2,1,0:T(8,128)(2,1)} %get-tuple-element.20), channel_id=1, source_target_pairs={{0,32},{32,0},{64,96},{96,64},{128,160},{160,128},{192,224},{224,1... | collective-permute-start | bytes 1572872 | tf_op jit(solution)/shard_map/ppermute | solution.py:147
  108.1 8.3 %collective-permute-start.5 = (bf16[8,128,256]{2,1,0:T(8,128)(2,1)S(1)}, bf16[8,128,256]{2,1,0:T(8,128)(2,1)S(1)}, u32[]{:S(2)}, u32[]{:S(2)}) collective-permute-start(bf16[8,128,256]{2,1,0:T(8,128)(2,1)S(1)} %all-to-all-done.4.mine_ref.after_ref), channel_id=1, source_target_pairs={{0,32},{32,0},{64,96},{96,64},{128,160},{160,128},{192,224},{224,1... | collective-permute-start | bytes 1572872 | tf_op jit(solution)/shard_map/ppermute | solution.py:147
  114.5 2.0 %copy-start.2 = (f32[8,128,256]{2,1,0:T(8,128)}, f32[8,128,256]{2,1,0:T(8,128)S(1)}, u32[]{:S(2)}) copy-start(f32[8,128,256]{2,1,0:T(8,128)S(1)} %convert_add_fusion) | copy-start | bytes 3145732
  114.5 16.6 %collective-permute-start.7 = (bf16[4,128,256]{2,1,0:T(8,128)(2,1)S(1)}, bf16[4,128,256]{2,1,0:T(8,128)(2,1)S(1)}, u32[]{:S(2)}, u32[]{:S(2)}) collective-permute-start(bf16[4,128,256]{2,1,0:T(8,128)(2,1)S(1)} %slice.112), channel_id=1, source_target_pairs={{0,128},{32,160},{64,192},{96,224},{128,0},{160,32},{192,64},{224,... | collective-permute-start | bytes 786440 | tf_op jit(solution)/shard_map/ppermute | solution.py:147
  118.4 12.7 %copy-start.3 = (f32[8,128,256]{2,1,0:T(8,128)S(1)}, f32[8,128,256]{2,1,0:T(8,128)}, u32[]{:S(2)}) copy-start(f32[8,128,256]{2,1,0:T(8,128)} %copy-done.2) | copy-start | bytes 3145732
  118.4 27.1 %all-to-all-start.5 = ((bf16[32,32,256]{2,1,0:T(8,128)(2,1)}), bf16[32,32,256]{2,1,0:T(8,128)(2,1)S(1)}, u32[]{:S(2)}, u32[]{:S(2)}) async-start(bf16[32,32,256]{2,1,0:T(8,128)(2,1)} %query_sums.3.after_ref), calls=%async_computation.5 | async-start | bytes 1048576 | tf_op jit(solution)/shard_map/all_to_all | solution.py:102
  131.2 11.4 %collective-permute-start.10 = (bf16[128,256]{1,0:T(8,128)(2,1)S(1)}, bf16[128,256]{1,0:T(8,128)(2,1)S(1)}, u32[]{:S(2)}, u32[]{:S(2)}) collective-permute-start(bf16[128,256]{1,0:T(8,128)(2,1)S(1)} %get-tuple-element.23), channel_id=1, source_target_pairs={{0,320},{32,352},{64,256},{96,288},{128,448},{160,480},{192,384},{... | collective-permute-start | bytes 196616 | tf_op jit(solution)/shard_map/ppermute | solution.py:210
  133.2 9.5 %collective-permute-start.8 = (bf16[128,256]{1,0:T(8,128)(2,1)S(1)}, bf16[128,256]{1,0:T(8,128)(2,1)S(1)}, u32[]{:S(2)}, u32[]{:S(2)}) collective-permute-start(bf16[128,256]{1,0:T(8,128)(2,1)S(1)} %get-tuple-element.21), channel_id=1, source_target_pairs={{0,256},{32,288},{64,320},{96,352},{128,384},{160,416},{192,448},{... | collective-permute-start | bytes 196616 | tf_op jit(solution)/shard_map/ppermute | solution.py:210
  136.4 8.4 %collective-permute-start.9 = (bf16[128,256]{1,0:T(8,128)(2,1)S(1)}, bf16[128,256]{1,0:T(8,128)(2,1)S(1)}, u32[]{:S(2)}, u32[]{:S(2)}) collective-permute-start(bf16[128,256]{1,0:T(8,128)(2,1)S(1)} %get-tuple-element.22), channel_id=1, source_target_pairs={{0,64},{32,96},{64,0},{96,32},{128,192},{160,224},{192,128},{224,1... | collective-permute-start | bytes 196616 | tf_op jit(solution)/shard_map/ppermute | solution.py:210

commit v5 on v4

--- a/solution.py
+++ b/solution.py
@@ -131,7 +131,7 @@
     rows = tile_rows % slab_blocks
     cols = tile_cols // n_ha
     slots = ((cols % 2) ^ core) * chips + cols // 2
-    halving_0, halving_1 = (0, 3, 1, 2), (0, 2, 1, 3)
+    halving_0, halving_1 = (0, 3, 1, 2), (0, 1, 3, 2)
     away = cols ^ lax.axis_index("pb")
     live = jnp.arange(CAP, dtype=jnp.int32) < live_tiles[0]
     keep = (keep_mask * live[None]).astype(jnp.float32)

time: 148 us -> 146 us (0.986)
  waiting for transfers between devices: 39.3 us -> 37.5 us
    ppermute x8, waiting for transfers between devices: 12.1 us -> 8.16 us  [swap(): return lax.ppermute(blocks, axis, [(i, i ^ 1 << bit) for i in range(size)])]
where the time goes in v5:
time: 146 us; the launch traced here: 145 us
  starting transfers between devices  90.1 us (62%)
  waiting for transfers between devices  37.5 us (26%)
  Pallas kernels  10.4 us (7%)
  other arithmetic  3.42 us (2%)
  between operations  1.69 us (1%)
  local copies, waits for them, and re-layouts  1.63 us (1%)
    all_to_all x6, starting transfers between devices, exchange(): lax.all_to_all(blocks, axis, 0, 0, axis_index_groups=groups, tiled=True)  46.8 us
    ppermute x8, starting transfers between devices, swap(): return lax.ppermute(blocks, axis, [(i, i ^ 1 << bit) for i in range(size)])  32 us
    all_to_all x6, waiting for transfers between devices, exchange(): lax.all_to_all(blocks, axis, 0, 0, axis_index_groups=groups, tiled=True)  26.3 us
    ppermute x3, starting transfers between devices, per_device(): other = lax.ppermute(block, 'pb', [(i, i ^ across) for i in range(n_pb)])  11.4 us
    ppermute x8, waiting for transfers between devices, swap(): return lax.ppermute(blocks, axis, [(i, i ^ 1 << bit) for i in range(size)])  8.16 us
    pallas_call x2, Pallas kernels, query_sums(): call(query_kernel, 'query_sums', half(n_ha, local, BOTH), [SMEM, SMEM, SM...  3.74 us
    pallas_call x2, Pallas kernels, host_sums(): call(host_kernel, 'host_sums', (single(chips, BLOCK, BOTH), half(chips, B...  3.23 us
    ppermute x3, waiting for transfers between devices, per_device(): other = lax.ppermute(block, 'pb', [(i, i ^ across) for i in range(n_pb)])  3.08 us
  transfers between devices with their start and end apart: 17, of which 11 were waited for; matrix products, arithmetic and copies ran while one was open for 1% of the time, Pallas kernels for 5%

profile of v5, /device:TPU:1, one launch (start us, length us, event | category | flops | bytes accessed | tf_op | source)
XLA Modules:
  0.0 144.8 jit_solution(17423411652130925194)
XLA Ops:
  2.8 7.7 %all-to-all-start = ((bf16[8,128,128]{2,1,0:T(8,128)(2,1)}), bf16[8,128,128]{2,1,0:T(8,128)(2,1)S(1)}, u32[]{:S(2)}, u32[]{:S(2)}) async-start(bf16[8,128,128]{2,1,0:T(8,128)(2,1)} %host_spread.1), calls=%async_computation | async-start | bytes 524288 | tf_op jit(solution)/shard_map/all_to_all | solution.py:102
  11.9 8.0 %all-to-all-done.mine_ref.after_ref = bf16[8,128,128]{2,1,0:T(8,128)(2,1)S(1)} async-done(((bf16[8,128,128]{2,1,0:T(8,128)(2,1)}), bf16[8,128,128]{2,1,0:T(8,128)(2,1)S(1)}, u32[]{:S(2)}, u32[]{:S(2)}) %all-to-all-start) | async-done | bytes 262176 | tf_op jit(solution)/shard_map/all_to_all | solution.py:102
  20.7 14.0 %all-to-all-start.2 = ((bf16[32,32,128]{2,1,0:T(8,128)(2,1)}), bf16[32,32,128]{2,1,0:T(8,128)(2,1)S(1)}, u32[]{:S(2)}, u32[]{:S(2)}) async-start(bf16[32,32,128]{2,1,0:T(8,128)(2,1)} %query_spread.1), calls=%async_computation.2 | async-start | bytes 524288 | tf_op jit(solution)/shard_map/all_to_all | solution.py:102
  34.7 4.7 %collective-permute-start = (bf16[8,128,128]{2,1,0:T(8,128)(2,1)S(1)}, bf16[8,128,128]{2,1,0:T(8,128)(2,1)S(1)}, u32[]{:S(2)}, u32[]{:S(2)}) collective-permute-start(bf16[8,128,128]{2,1,0:T(8,128)(2,1)S(1)} %all-to-all-done.mine_ref.after_ref), channel_id=1, source_target_pairs={{0,32},{32,0},{64,96},{96,64},{128,160},{160,128},{192,224},{224,1... | collective-permute-start | bytes 786440 | tf_op jit(solution)/shard_map/ppermute | solution.py:147
  40.5 1.8 %query_sums.2.after_ref = bf16[32,32,256]{2,1,0:T(8,128)(2,1)} custom-call(s32[16]{0:T(128)S(1)} %get-tuple-element.40.rows_ref, s32[16]{0:T(128)S(1)} %get-tuple-element.39.slots_ref, f32[2,16]{1,0:T(2,128)S(1)} %multiply_convert_fusion.3.keep_ref, bf16[16,128,128]{2,1,0:T(8,128)(2,1)S(1)} %convert_element_type.87.w_ref, ...), custom_call_target="tpu_custom_call" | custom-call | flops 67108864 | bytes 2097152 | tf_op jit(solution)/shard_map/query_sums/pallas_call | solution.py:163
  42.4 2.8 %all-to-all-done.2.q_ref = bf16[32,32,128]{2,1,0:T(8,128)(2,1)S(1)} async-done(((bf16[32,32,128]{2,1,0:T(8,128)(2,1)}), bf16[32,32,128]{2,1,0:T(8,128)(2,1)S(1)}, u32[]{:S(2)}, u32[]{:S(2)}) %all-to-all-start.2) | async-done | bytes 262176 | tf_op jit(solution)/shard_map/all_to_all | solution.py:102
  45.2 6.7 %all-to-all-start.1 = ((bf16[32,32,256]{2,1,0:T(8,128)(2,1)}), bf16[32,32,256]{2,1,0:T(8,128)(2,1)S(1)}, u32[]{:S(2)}, u32[]{:S(2)}) async-start(bf16[32,32,256]{2,1,0:T(8,128)(2,1)} %query_sums.2.after_ref), calls=%async_computation.1 | async-start | bytes 1048576 | tf_op jit(solution)/shard_map/all_to_all | solution.py:102
  51.9 1.2 host_sums.2
  53.1 3.0 %collective-permute-start.1 = (bf16[8,128,256]{2,1,0:T(8,128)(2,1)S(1)}, bf16[8,128,256]{2,1,0:T(8,128)(2,1)S(1)}, u32[]{:S(2)}, u32[]{:S(2)}) collective-permute-start(bf16[8,128,256]{2,1,0:T(8,128)(2,1)S(1)} %get-tuple-element.14), channel_id=1, source_target_pairs={{0,32},{32,0},{64,96},{96,64},{128,160},{160,128},{192,224},{224,1... | collective-permute-start | bytes 1572872 | tf_op jit(solution)/shard_map/ppermute | solution.py:147
  56.1 1.5 %collective-permute-done.1 = bf16[8,128,256]{2,1,0:T(8,128)(2,1)S(1)} collective-permute-done((bf16[8,128,256]{2,1,0:T(8,128)(2,1)S(1)}, bf16[8,128,256]{2,1,0:T(8,128)(2,1)S(1)}, u32[]{:S(2)}, u32[]{:S(2)}) %collective-permute-start.1) | collective-permute-done | bytes 524320 | tf_op jit(solution)/shard_map/ppermute | solution.py:147
  57.8 2.9 %collective-permute-start.2 = (bf16[4,128,256]{2,1,0:T(8,128)(2,1)S(1)}, bf16[4,128,256]{2,1,0:T(8,128)(2,1)S(1)}, u32[]{:S(2)}, u32[]{:S(2)}) collective-permute-start(bf16[4,128,256]{2,1,0:T(8,128)(2,1)S(1)} %slice.113), channel_id=1, source_target_pairs={{0,256},{32,288},{64,320},{96,352},{128,384},{160,416},{192,448},{... | collective-permute-start | bytes 786440 | tf_op jit(solution)/shard_map/ppermute | solution.py:147
  60.7 6.7 %all-to-all-done.1.in_ref = bf16[32,32,256]{2,1,0:T(8,128)(2,1)S(1)} async-done(((bf16[32,32,256]{2,1,0:T(8,128)(2,1)}), bf16[32,32,256]{2,1,0:T(8,128)(2,1)S(1)}, u32[]{:S(2)}, u32[]{:S(2)}) %all-to-all-start.1) | async-done | bytes 524320 | tf_op jit(solution)/shard_map/all_to_all | solution.py:102
  67.4 0.9 query_update.1
  68.3 5.9 %all-to-all-start.3 = ((bf16[32,32,256]{2,1,0:T(8,128)(2,1)}), bf16[32,32,256]{2,1,0:T(8,128)(2,1)S(1)}, u32[]{:S(2)}, u32[]{:S(2)}) async-start(bf16[32,32,256]{2,1,0:T(8,128)(2,1)} %get-tuple-element.16), calls=%async_computation.3 | async-start | bytes 1048576 | tf_op jit(solution)/shard_map/all_to_all | solution.py:102
  74.4 5.5 %collective-permute-start.3 = (bf16[2,128,256]{2,1,0:T(8,128)(2,1)S(1)}, bf16[2,128,256]{2,1,0:T(8,128)(2,1)S(1)}, u32[]{:S(2)}, u32[]{:S(2)}) collective-permute-start(bf16[2,128,256]{2,1,0:T(8,128)(2,1)S(1)} %slice.114), channel_id=1, source_target_pairs={{0,64},{32,96},{64,0},{96,32},{128,192},{160,224},{192,128},{224,1... | collective-permute-start | bytes 393224 | tf_op jit(solution)/shard_map/ppermute | solution.py:147
  79.8 2.3 %collective-permute-done.3 = bf16[2,128,256]{2,1,0:T(8,128)(2,1)S(1)} collective-permute-done((bf16[2,128,256]{2,1,0:T(8,128)(2,1)S(1)}, bf16[2,128,256]{2,1,0:T(8,128)(2,1)S(1)}, u32[]{:S(2)}, u32[]{:S(2)}) %collective-permute-start.3) | collective-permute-done | bytes 131104 | tf_op jit(solution)/shard_map/ppermute | solution.py:147
  82.2 2.2 %collective-permute-start.4 = (bf16[1,128,256]{2,1,0:T(8,128)(2,1)S(1)}, bf16[1,128,256]{2,1,0:T(8,128)(2,1)S(1)}, u32[]{:S(2)}, u32[]{:S(2)}) collective-permute-start(bf16[1,128,256]{2,1,0:T(8,128)(2,1)S(1)} %slice.115), channel_id=1, source_target_pairs={{0,128},{32,160},{64,192},{96,224},{128,0},{160,32},{192,64},{224,... | collective-permute-start | bytes 196616 | tf_op jit(solution)/shard_map/ppermute | solution.py:147
  84.5 4.0 %collective-permute-done.4 = bf16[1,128,256]{2,1,0:T(8,128)(2,1)S(1)} collective-permute-done((bf16[1,128,256]{2,1,0:T(8,128)(2,1)S(1)}, bf16[1,128,256]{2,1,0:T(8,128)(2,1)S(1)}, u32[]{:S(2)}, u32[]{:S(2)}) %collective-permute-start.4) | collective-permute-done | bytes 65568 | tf_op jit(solution)/shard_map/ppermute | solution.py:147
  89.3 0.9 host_update.1
  90.2 3.8 %all-to-all-start.4 = ((bf16[8,128,256]{2,1,0:T(8,128)(2,1)}), bf16[8,128,256]{2,1,0:T(8,128)(2,1)S(1)}, u32[]{:S(2)}, u32[]{:S(2)}) async-start(bf16[8,128,256]{2,1,0:T(8,128)(2,1)} %get-tuple-element.17.after_ref), calls=%async_computation.4 | async-start | bytes 1048576 | tf_op jit(solution)/shard_map/all_to_all | solution.py:102
  94.0 2.0 %host_sums.3 = (f32[8,128,256]{2,1,0:T(8,128)S(1)}, bf16[8,128,256]{2,1,0:T(8,128)(2,1)}) custom-call(s32[16]{0:T(128)S(1)} %get-tuple-element.40.rows_ref, s32[16]{0:T(128)S(1)} %get-tuple-element.24.slots_ref, f32[2,16]{1,0:T(2,128)S(1)} %multiply_convert_fusion.3.keep_ref, bf16[16,128,128]{2,1,0:T(8,128)(2,1)S(1)} %convert_element_type.87.w_ref, ...), custom_call_target="tpu_custom_call" | custom-call | flops 134217728 | bytes 2097152 | tf_op jit(solution)/shard_map/host_sums/pallas_call | solution.py:153
  96.0 5.4 %collective-permute-start.6 = (bf16[8,128,256]{2,1,0:T(8,128)(2,1)}, bf16[8,128,256]{2,1,0:T(8,128)(2,1)S(1)}, u32[]{:S(2)}, u32[]{:S(2)}) collective-permute-start(bf16[8,128,256]{2,1,0:T(8,128)(2,1)} %get-tuple-element.20), channel_id=1, source_target_pairs={{0,32},{32,0},{64,96},{96,64},{128,160},{160,128},{192,224},{224,1... | collective-permute-start | bytes 1572872 | tf_op jit(solution)/shard_map/ppermute | solution.py:147
  101.4 6.7 %all-to-all-done.4.mine_ref.after_ref = bf16[8,128,256]{2,1,0:T(8,128)(2,1)S(1)} async-done(((bf16[8,128,256]{2,1,0:T(8,128)(2,1)}), bf16[8,128,256]{2,1,0:T(8,128)(2,1)S(1)}, u32[]{:S(2)}, u32[]{:S(2)}) %all-to-all-start.4) | async-done | bytes 524320 | tf_op jit(solution)/shard_map/all_to_all | solution.py:102
  108.1 6.2 %collective-permute-start.5 = (bf16[8,128,256]{2,1,0:T(8,128)(2,1)S(1)}, bf16[8,128,256]{2,1,0:T(8,128)(2,1)S(1)}, u32[]{:S(2)}, u32[]{:S(2)}) collective-permute-start(bf16[8,128,256]{2,1,0:T(8,128)(2,1)S(1)} %all-to-all-done.4.mine_ref.after_ref), channel_id=1, source_target_pairs={{0,32},{32,0},{64,96},{96,64},{128,160},{160,128},{192,224},{224,1... | collective-permute-start | bytes 1572872 | tf_op jit(solution)/shard_map/ppermute | solution.py:147
  114.5 2.2 %collective-permute-start.7 = (bf16[4,128,256]{2,1,0:T(8,128)(2,1)S(1)}, bf16[4,128,256]{2,1,0:T(8,128)(2,1)S(1)}, u32[]{:S(2)}, u32[]{:S(2)}) collective-permute-start(bf16[4,128,256]{2,1,0:T(8,128)(2,1)S(1)} %slice.112), channel_id=1, source_target_pairs={{0,64},{32,96},{64,0},{96,32},{128,192},{160,224},{192,128},{224,1... | collective-permute-start | bytes 786440 | tf_op jit(solution)/shard_map/ppermute | solution.py:147
  116.8 1.9 %query_sums.3.after_ref = bf16[32,32,256]{2,1,0:T(8,128)(2,1)} custom-call(s32[16]{0:T(128)S(1)} %get-tuple-element.40.rows_ref, s32[16]{0:T(128)S(1)} %get-tuple-element.39.slots_ref, f32[2,16]{1,0:T(2,128)S(1)} %multiply_convert_fusion.3.keep_ref, bf16[16,128,128]{2,1,0:T(8,128)(2,1)S(1)} %convert_element_type.87.w_ref, ...), custom_call_target="tpu_custom_call" | custom-call | flops 134217728 | bytes 2097152 | tf_op jit(solution)/shard_map/query_sums/pallas_call | solution.py:163
  118.7 8.8 %all-to-all-start.5 = ((bf16[32,32,256]{2,1,0:T(8,128)(2,1)}), bf16[32,32,256]{2,1,0:T(8,128)(2,1)S(1)}, u32[]{:S(2)}, u32[]{:S(2)}) async-start(bf16[32,32,256]{2,1,0:T(8,128)(2,1)} %query_sums.3.after_ref), calls=%async_computation.5 | async-start | bytes 1048576 | tf_op jit(solution)/shard_map/all_to_all | solution.py:102
  127.6 1.9 %collective-permute-start.10 = (bf16[128,256]{1,0:T(8,128)(2,1)S(1)}, bf16[128,256]{1,0:T(8,128)(2,1)S(1)}, u32[]{:S(2)}, u32[]{:S(2)}) collective-permute-start(bf16[128,256]{1,0:T(8,128)(2,1)S(1)} %get-tuple-element.23), channel_id=1, source_target_pairs={{0,384},{32,416},{64,448},{96,480},{128,256},{160,288},{192,320},{... | collective-permute-start | bytes 196616 | tf_op jit(solution)/shard_map/ppermute | solution.py:210
  129.5 3.4 %collective-permute-start.8 = (bf16[128,256]{1,0:T(8,128)(2,1)S(1)}, bf16[128,256]{1,0:T(8,128)(2,1)S(1)}, u32[]{:S(2)}, u32[]{:S(2)}) collective-permute-start(bf16[128,256]{1,0:T(8,128)(2,1)S(1)} %get-tuple-element.21), channel_id=1, source_target_pairs={{0,128},{32,160},{64,192},{96,224},{128,0},{160,32},{192,64},{224,... | collective-permute-start | bytes 196616 | tf_op jit(solution)/shard_map/ppermute | solution.py:210
  132.9 6.1 %collective-permute-start.9 = (bf16[128,256]{1,0:T(8,128)(2,1)S(1)}, bf16[128,256]{1,0:T(8,128)(2,1)S(1)}, u32[]{:S(2)}, u32[]{:S(2)}) collective-permute-start(bf16[128,256]{1,0:T(8,128)(2,1)S(1)} %get-tuple-element.22), channel_id=1, source_target_pairs={{0,256},{32,288},{64,320},{96,352},{128,384},{160,416},{192,448},{... | collective-permute-start | bytes 196616 | tf_op jit(solution)/shard_map/ppermute | solution.py:210
  139.0 3.1 %collective-permute-done.9 = bf16[128,256]{1,0:T(8,128)(2,1)S(1)} collective-permute-done((bf16[128,256]{1,0:T(8,128)(2,1)S(1)}, bf16[128,256]{1,0:T(8,128)(2,1)S(1)}, u32[]{:S(2)}, u32[]{:S(2)}) %collective-permute-start.9) | collective-permute-done | bytes 65568 | tf_op jit(solution)/shard_map/ppermute | solution.py:210
  142.9 1.2 all-to-all-done.5
  (57 shorter events, 7.8 us)
Async XLA Ops:
  1.3 0.8 copy-start
  1.3 0.8 copy-start.1
  1.3 38.1 %copy-start.4 = (s32[16,128,128]{2,1,0:T(8,128)S(1)}, s32[16,128,128]{2,1,0:T(8,128)}, u32[]{:S(2)}) copy-start(s32[16,128,128]{2,1,0:T(8,128)} %param.15) | copy-start | bytes 3145732
  2.8 17.1 %all-to-all-start = ((bf16[8,128,128]{2,1,0:T(8,128)(2,1)}), bf16[8,128,128]{2,1,0:T(8,128)(2,1)S(1)}, u32[]{:S(2)}, u32[]{:S(2)}) async-start(bf16[8,128,128]{2,1,0:T(8,128)(2,1)} %host_spread.1), calls=%async_computation | async-start | bytes 524288 | tf_op jit(solution)/shard_map/all_to_all | solution.py:102
  20.7 14.0 %copy-start.5 = (s32[2,16]{1,0:T(2,128)S(1)}, s32[2,16]{1,0:T(2,128)}, u32[]{:S(2)}) copy-start(s32[2,16]{1,0:T(2,128)} %param.16) | copy-start | bytes 388
  20.7 24.5 %all-to-all-start.2 = ((bf16[32,32,128]{2,1,0:T(8,128)(2,1)}), bf16[32,32,128]{2,1,0:T(8,128)(2,1)S(1)}, u32[]{:S(2)}, u32[]{:S(2)}) async-start(bf16[32,32,128]{2,1,0:T(8,128)(2,1)} %query_spread.1), calls=%async_computation.2 | async-start | bytes 524288 | tf_op jit(solution)/shard_map/all_to_all | solution.py:102
  34.7 4.7 %copy-start.7 = (s32[16]{0:T(128)S(1)}, s32[16]{0:T(128)}, u32[]{:S(2)}) copy-start(s32[16]{0:T(128)} %param.14) | copy-start | bytes 196
  34.7 5.8 %collective-permute-start = (bf16[8,128,128]{2,1,0:T(8,128)(2,1)S(1)}, bf16[8,128,128]{2,1,0:T(8,128)(2,1)S(1)}, u32[]{:S(2)}, u32[]{:S(2)}) collective-permute-start(bf16[8,128,128]{2,1,0:T(8,128)(2,1)S(1)} %all-to-all-done.mine_ref.after_ref), channel_id=1, source_target_pairs={{0,32},{32,0},{64,96},{96,64},{128,160},{160,128},{192,224},{224,1... | collective-permute-start | bytes 786440 | tf_op jit(solution)/shard_map/ppermute | solution.py:147
  39.6 0.7 copy-start.6
  45.2 22.2 %all-to-all-start.1 = ((bf16[32,32,256]{2,1,0:T(8,128)(2,1)}), bf16[32,32,256]{2,1,0:T(8,128)(2,1)S(1)}, u32[]{:S(2)}, u32[]{:S(2)}) async-start(bf16[32,32,256]{2,1,0:T(8,128)(2,1)} %query_sums.2.after_ref), calls=%async_computation.1 | async-start | bytes 1048576 | tf_op jit(solution)/shard_map/all_to_all | solution.py:102
  53.1 4.5 %collective-permute-start.1 = (bf16[8,128,256]{2,1,0:T(8,128)(2,1)S(1)}, bf16[8,128,256]{2,1,0:T(8,128)(2,1)S(1)}, u32[]{:S(2)}, u32[]{:S(2)}) collective-permute-start(bf16[8,128,256]{2,1,0:T(8,128)(2,1)S(1)} %get-tuple-element.14), channel_id=1, source_target_pairs={{0,32},{32,0},{64,96},{96,64},{128,160},{160,128},{192,224},{224,1... | collective-permute-start | bytes 1572872 | tf_op jit(solution)/shard_map/ppermute | solution.py:147
  57.8 16.5 %collective-permute-start.2 = (bf16[4,128,256]{2,1,0:T(8,128)(2,1)S(1)}, bf16[4,128,256]{2,1,0:T(8,128)(2,1)S(1)}, u32[]{:S(2)}, u32[]{:S(2)}) collective-permute-start(bf16[4,128,256]{2,1,0:T(8,128)(2,1)S(1)} %slice.113), channel_id=1, source_target_pairs={{0,256},{32,288},{64,320},{96,352},{128,384},{160,416},{192,448},{... | collective-permute-start | bytes 786440 | tf_op jit(solution)/shard_map/ppermute | solution.py:147
  68.3 21.0 %all-to-all-start.3 = ((bf16[32,32,256]{2,1,0:T(8,128)(2,1)}), bf16[32,32,256]{2,1,0:T(8,128)(2,1)S(1)}, u32[]{:S(2)}, u32[]{:S(2)}) async-start(bf16[32,32,256]{2,1,0:T(8,128)(2,1)} %get-tuple-element.16), calls=%async_computation.3 | async-start | bytes 1048576 | tf_op jit(solution)/shard_map/all_to_all | solution.py:102
  74.4 7.8 %collective-permute-start.3 = (bf16[2,128,256]{2,1,0:T(8,128)(2,1)S(1)}, bf16[2,128,256]{2,1,0:T(8,128)(2,1)S(1)}, u32[]{:S(2)}, u32[]{:S(2)}) collective-permute-start(bf16[2,128,256]{2,1,0:T(8,128)(2,1)S(1)} %slice.114), channel_id=1, source_target_pairs={{0,64},{32,96},{64,0},{96,32},{128,192},{160,224},{192,128},{224,1... | collective-permute-start | bytes 393224 | tf_op jit(solution)/shard_map/ppermute | solution.py:147
  82.2 6.2 %collective-permute-start.4 = (bf16[1,128,256]{2,1,0:T(8,128)(2,1)S(1)}, bf16[1,128,256]{2,1,0:T(8,128)(2,1)S(1)}, u32[]{:S(2)}, u32[]{:S(2)}) collective-permute-start(bf16[1,128,256]{2,1,0:T(8,128)(2,1)S(1)} %slice.115), channel_id=1, source_target_pairs={{0,128},{32,160},{64,192},{96,224},{128,0},{160,32},{192,64},{224,... | collective-permute-start | bytes 196616 | tf_op jit(solution)/shard_map/ppermute | solution.py:147
  90.2 17.9 %all-to-all-start.4 = ((bf16[8,128,256]{2,1,0:T(8,128)(2,1)}), bf16[8,128,256]{2,1,0:T(8,128)(2,1)S(1)}, u32[]{:S(2)}, u32[]{:S(2)}) async-start(bf16[8,128,256]{2,1,0:T(8,128)(2,1)} %get-tuple-element.17.after_ref), calls=%async_computation.4 | async-start | bytes 1048576 | tf_op jit(solution)/shard_map/all_to_all | solution.py:102
  96.0 18.3 %collective-permute-start.6 = (bf16[8,128,256]{2,1,0:T(8,128)(2,1)}, bf16[8,128,256]{2,1,0:T(8,128)(2,1)S(1)}, u32[]{:S(2)}, u32[]{:S(2)}) collective-permute-start(bf16[8,128,256]{2,1,0:T(8,128)(2,1)} %get-tuple-element.20), channel_id=1, source_target_pairs={{0,32},{32,0},{64,96},{96,64},{128,160},{160,128},{192,224},{224,1... | collective-permute-start | bytes 1572872 | tf_op jit(solution)/shard_map/ppermute | solution.py:147
  108.1 8.6 %collective-permute-start.5 = (bf16[8,128,256]{2,1,0:T(8,128)(2,1)S(1)}, bf16[8,128,256]{2,1,0:T(8,128)(2,1)S(1)}, u32[]{:S(2)}, u32[]{:S(2)}) collective-permute-start(bf16[8,128,256]{2,1,0:T(8,128)(2,1)S(1)} %all-to-all-done.4.mine_ref.after_ref), channel_id=1, source_target_pairs={{0,32},{32,0},{64,96},{96,64},{128,160},{160,128},{192,224},{224,1... | collective-permute-start | bytes 1572872 | tf_op jit(solution)/shard_map/ppermute | solution.py:147
  114.5 2.3 %copy-start.2 = (f32[8,128,256]{2,1,0:T(8,128)}, f32[8,128,256]{2,1,0:T(8,128)S(1)}, u32[]{:S(2)}) copy-start(f32[8,128,256]{2,1,0:T(8,128)S(1)} %convert_add_fusion) | copy-start | bytes 3145732
  114.5 12.9 %collective-permute-start.7 = (bf16[4,128,256]{2,1,0:T(8,128)(2,1)S(1)}, bf16[4,128,256]{2,1,0:T(8,128)(2,1)S(1)}, u32[]{:S(2)}, u32[]{:S(2)}) collective-permute-start(bf16[4,128,256]{2,1,0:T(8,128)(2,1)S(1)} %slice.112), channel_id=1, source_target_pairs={{0,64},{32,96},{64,0},{96,32},{128,192},{160,224},{192,128},{224,1... | collective-permute-start | bytes 786440 | tf_op jit(solution)/shard_map/ppermute | solution.py:147
  118.7 8.8 %copy-start.3 = (f32[8,128,256]{2,1,0:T(8,128)S(1)}, f32[8,128,256]{2,1,0:T(8,128)}, u32[]{:S(2)}) copy-start(f32[8,128,256]{2,1,0:T(8,128)} %copy-done.2) | copy-start | bytes 3145732
  118.7 25.4 %all-to-all-start.5 = ((bf16[32,32,256]{2,1,0:T(8,128)(2,1)}), bf16[32,32,256]{2,1,0:T(8,128)(2,1)S(1)}, u32[]{:S(2)}, u32[]{:S(2)}) async-start(bf16[32,32,256]{2,1,0:T(8,128)(2,1)} %query_sums.3.after_ref), calls=%async_computation.5 | async-start | bytes 1048576 | tf_op jit(solution)/shard_map/all_to_all | solution.py:102
  127.6 11.4 %collective-permute-start.10 = (bf16[128,256]{1,0:T(8,128)(2,1)S(1)}, bf16[128,256]{1,0:T(8,128)(2,1)S(1)}, u32[]{:S(2)}, u32[]{:S(2)}) collective-permute-start(bf16[128,256]{1,0:T(8,128)(2,1)S(1)} %get-tuple-element.23), channel_id=1, source_target_pairs={{0,384},{32,416},{64,448},{96,480},{128,256},{160,288},{192,320},{... | collective-permute-start | bytes 196616 | tf_op jit(solution)/shard_map/ppermute | solution.py:210
  129.5 9.5 %collective-permute-start.8 = (bf16[128,256]{1,0:T(8,128)(2,1)S(1)}, bf16[128,256]{1,0:T(8,128)(2,1)S(1)}, u32[]{:S(2)}, u32[]{:S(2)}) collective-permute-start(bf16[128,256]{1,0:T(8,128)(2,1)S(1)} %get-tuple-element.21), channel_id=1, source_target_pairs={{0,128},{32,160},{64,192},{96,224},{128,0},{160,32},{192,64},{224,... | collective-permute-start | bytes 196616 | tf_op jit(solution)/shard_map/ppermute | solution.py:210
  132.9 9.2 %collective-permute-start.9 = (bf16[128,256]{1,0:T(8,128)(2,1)S(1)}, bf16[128,256]{1,0:T(8,128)(2,1)S(1)}, u32[]{:S(2)}, u32[]{:S(2)}) collective-permute-start(bf16[128,256]{1,0:T(8,128)(2,1)S(1)} %get-tuple-element.22), channel_id=1, source_target_pairs={{0,256},{32,288},{64,320},{96,352},{128,384},{160,416},{192,448},{... | collective-permute-start | bytes 196616 | tf_op jit(solution)/shard_map/ppermute | solution.py:210
